TPU v7x, 32 devices: a whole 2x2x4 slice. The times are simulated.
32 devices in a mesh: fsdp: 4 (over z), context: 2 (over y), tensor: 4 (over x, core).
Axes of the slice: x: 2, y: 2, z: 4, core: 2. Of those that a mesh axis runs over, the one named last changes fastest.
Arguments:
- tokens: bfloat16 [4, 2048, 1536], P('fsdp', ('context', 'tensor')), may hold values from -6 to 6
- cotangent: bfloat16 [4, 2048, 1536], P('fsdp', ('context', 'tensor')), may hold values from -6 to 6
- segment_ids: int32 [4, 2048], P('fsdp'), may hold values from 0 to 511, as said below
- w_query: bfloat16 [1536, 1536], P(('fsdp', 'context'), 'tensor'), may hold values from -0.15625 to 0.15625
- w_keyval: bfloat16 [1536, 256], P(('fsdp', 'context', 'tensor')), may hold values from -0.15625 to 0.15625
- w_out: bfloat16 [1536, 1536], P('tensor', ('fsdp', 'context')), may hold values from -0.875 to 0.875
- w_gate: bfloat16 [1536, 4608], P(('fsdp', 'context'), 'tensor'), may hold values from -0.15625 to 0.15625
- w_up: bfloat16 [1536, 4608], P(('fsdp', 'context'), 'tensor'), may hold values from -0.15625 to 0.15625
- contract_factor: bfloat16 [4608, 1536], P('tensor', ('fsdp', 'context')), may hold values from -0.09375 to 0.09375
- norm_gains: bfloat16 [2, 1536], P(None, ('fsdp', 'context', 'tensor')), may hold values from 0.099609375 to 1.8984375
Outputs:
- output: bfloat16 [4, 2048, 1536], P('fsdp', ('context', 'tensor'))
- input_grad: float32 [4, 2048, 1536], P('fsdp', ('context', 'tensor'))
- grad_query: float32 [1536, 1536], P(('fsdp', 'context'), 'tensor')
- grad_keyval: float32 [1536, 256], P(('fsdp', 'context', 'tensor'))
- grad_out: float32 [1536, 1536], P('tensor', ('fsdp', 'context'))
- grad_gate: float32 [1536, 4608], P(('fsdp', 'context'), 'tensor')
- grad_up: float32 [1536, 4608], P(('fsdp', 'context'), 'tensor')
- grad_down: float32 [4608, 1536], P('tensor', ('fsdp', 'context'))
- grad_gains: float32 [2, 1536], P(None, ('fsdp', 'context', 'tensor'))
Inputs may be any that keep to these rules, and one draw needn't show every extreme that they name: `segment_ids`: along each sequence the ids start at 0 and rise by one where a new document begins; every document but a sequence's last holds 4 tokens or more and up to 2048; one of the sequences is a single document, and another is cut into documents of 4 tokens each.
All inputs are finite; a program needn't handle non-finite values.
Results may differ from a plain program's by a relative error of at most 0.015.
Values may be sent and summed in bfloat16 or wider, within the bound.
No kernel may reach another device: no remote copies, remote signals or barrier semaphores. Data moves between devices by JAX's collectives and lax.ppermute only.
A program may use at most 192 MiB of HBM per device.

v0:
```python
import functools

import jax
import jax.numpy as jnp
from jax import lax
from jax.experimental import pallas as pl
from jax.experimental.pallas import tpu as pltpu
from jax.sharding import PartitionSpec as P

HEAD_DIM = 128
WINDOW = 1024
EPSILON = 1e-06
LOG2E = 1.4426950408889634
SCALE = HEAD_DIM**-0.5
BF = jnp.bfloat16
F32 = jnp.float32


def swap(value, axis, k):
    count = lax.axis_size(axis)
    return lax.ppermute(value, axis, [(i, i ^ k) for i in range(count)])


def shift(value, axis, steps):
    count = lax.axis_size(axis)
    leading, last = max(0, -steps), min(count, count - steps)
    return lax.ppermute(value, axis, [(i, i + steps) for i in range(leading, last)])


def bits_of(count):
    return [1 << b for b in range(count.bit_length() - 1)]


def tensor_order(count):
    order = [0]
    for bit in reversed(bits_of(count)):
        order = order + [k ^ bit for k in order]
    return order


def after(value, *deps):
    return lax.optimization_barrier((value,) + deps)[0]


def tensor_blocks(value, first=(), later=()):
    pieces = behind([value], *first)
    bits = list(reversed(bits_of(lax.axis_size("tensor"))))
    for n, bit in enumerate(bits):
        if n == len(bits) - 1 and later:
            pieces = behind(pieces, *later)
        pieces = pieces + [swap(p, "tensor", bit) for p in pieces]
    return pieces


def reduce_halves(away, own):
    bits = bits_of(lax.axis_size("tensor"))
    back = swap(away.astype(BF), "tensor", bits[0])
    total = own + back.astype(F32)
    for bit in bits[1:]:
        half = total.shape[0] // 2
        back = swap(total[half:].astype(BF), "tensor", bit)
        total = total[:half] + back.astype(F32)
    return total


def reduce_tensor(make, rows):
    half = rows // 2
    return reduce_halves(make(half, rows), make(0, half))


def behind(values, *deps):
    return list(lax.optimization_barrier((tuple(values), deps))[0])


def across(value, *deps):
    (value,) = behind([value], *deps)
    return [swap(value, "context", k) for k in range(1, lax.axis_size("context"))]


def along(value, *deps):
    (value,) = behind([value], *deps)
    return [swap(value, "fsdp", k) for k in range(1, lax.axis_size("fsdp"))]


def place_kernel(cuts, slots, *refs):
    n_out = len(cuts)
    ins, outs, sems = refs[: -n_out - 1], refs[-n_out - 1 : -1], refs[-1]
    copies, n = [], 0
    for ref in ins:
        for i in range(ref.shape[0]):
            for out, (first, last) in zip(outs, cuts):
                copies.append(pltpu.make_async_copy(ref.at[i, first:last], out.at[slots[n]], sems.at[len(copies)]))
                copies[-1].start()
            n += 1
    for copy in copies:
        copy.wait()


def place(slots, pieces, cuts=None):
    count = sum(p.shape[0] for p in pieces)
    rows, n = pieces[0].shape[1:]
    cuts = cuts or [(0, rows)]
    anywhere = pl.BlockSpec(memory_space=pl.ANY)
    shapes = [(count, last - first, n) for first, last in cuts]
    out = pl.pallas_call(
        functools.partial(place_kernel, cuts),
        grid_spec=pltpu.PrefetchScalarGridSpec(
            num_scalar_prefetch=1,
            grid=(1,),
            in_specs=[anywhere] * len(pieces),
            out_specs=[whole_spec(shape) for shape in shapes],
            scratch_shapes=[pltpu.SemaphoreType.DMA((count * len(cuts),))],
        ),
        out_shape=[jax.ShapeDtypeStruct(shape, pieces[0].dtype) for shape in shapes],
        cost_estimate=pl.CostEstimate(flops=1, bytes_accessed=1, transcendentals=0),
        name="place",
    )(slots, *pieces)
    return [x.reshape(-1, n) for x in out]


def gathered(own, others, early, later):
    pieces = [own[None], others]
    for e, a in zip(early, later):
        pieces += [e[None], a]
    return pieces


def slots_of():
    nf, nc = lax.axis_size("fsdp"), lax.axis_size("context")
    f, c = lax.axis_index("fsdp"), lax.axis_index("context")
    js = jnp.array([j for _ in range(nc) for j in range(nf)], jnp.int32)
    ks = jnp.array([k for k in range(nc) for _ in range(nf)], jnp.int32)
    return (js ^ f) * nc + (ks ^ c)


def away_half(slabs):
    c = lax.axis_index("context")
    return [lax.dynamic_index_in_dim(slabs, c ^ k, 1, False) for k in range(1, lax.axis_size("context"))]


def half_sent(slabs, *deps):
    sent = behind(away_half(slabs), *deps)
    return [swap(x, "context", k + 1) for k, x in enumerate(sent)]


def half_sum(slabs, got):
    return lax.dynamic_index_in_dim(slabs, lax.axis_index("context"), 1, False).astype(F32) + sum(x.astype(F32) for x in got)


def rest_large(total):
    return lax.psum_scatter(total.astype(BF), "fsdp", scatter_dimension=0, tiled=False).astype(F32)


def rest_small(total, *deps):
    nf, f = lax.axis_size("fsdp"), lax.axis_index("fsdp")
    away = behind([lax.dynamic_index_in_dim(total, f ^ k, 0, False).astype(BF) for k in range(1, nf)], *deps)
    back = [swap(x, "fsdp", k + 1) for k, x in enumerate(away)]
    return lax.dynamic_index_in_dim(total, f, 0, False) + sum(x.astype(F32) for x in back), back


def slabs_of(part):
    nf, nc = lax.axis_size("fsdp"), lax.axis_size("context")
    return part.reshape(nf, nc, part.shape[0] // (nf * nc), part.shape[1])


def dot_nt(a, b):
    return lax.dot_general(a, b, (((1,), (1,)), ((), ())), preferred_element_type=F32)


def dot_nn(a, b):
    return lax.dot_general(a, b, (((1,), (0,)), ((), ())), preferred_element_type=F32)


def in_order(blocks_ref, prev_ref, own_ref, both, count, rows):
    for r in range(count):
        at = blocks_ref[r] * rows
        both[pl.ds(at, rows), :] = prev_ref[r * rows : (r + 1) * rows, :]
        both[pl.ds(at + count * rows, rows), :] = own_ref[r * rows : (r + 1) * rows, :]


def fill_bias(a, rows, count, qseg_ref, kseg_ref, bias, tri):
    qs = qseg_ref[...]
    wide = rows // 128

    def seg(i):
        s = kseg_ref[pl.ds((a + i) * rows, rows), :]
        return jnp.concatenate([s] * wide, axis=1) == qs

    first = (tri & seg(count)) | (jnp.logical_not(tri) & seg(0))
    bias[0] = jnp.where(first, 0.0, -1e30).astype(F32)
    for i in range(1, count):
        bias[i] = jnp.where(seg(i), 0.0, -1e30).astype(F32)


def attend_forward(blocks_ref, q_ref, prev_ref, own_ref, qseg_ref, kseg_ref, out_ref, lse_ref, both, vt, bias):
    count, rows, heads = bias.shape[0], q_ref.shape[0], q_ref.shape[1] // HEAD_DIM
    r = pl.program_id(0)
    a = blocks_ref[r]

    @pl.when(r == 0)
    def _():
        in_order(blocks_ref, prev_ref, own_ref, both, count, rows)
        for i in range(2 * count):
            vt[:, i * rows : (i + 1) * rows] = both[i * rows : (i + 1) * rows, HEAD_DIM:].T

    tri = lax.broadcasted_iota(jnp.int32, (rows, rows), 0) <= lax.broadcasted_iota(jnp.int32, (rows, rows), 1)
    fill_bias(a, rows, count, qseg_ref, kseg_ref, bias, tri)
    starts = [pl.multiple_of((a + i) * rows, rows) for i in range(count + 1)]
    for h in range(heads):
        q = q_ref[:, h * HEAD_DIM : (h + 1) * HEAD_DIM]
        s = [dot_nt(both[pl.ds(st, rows), :HEAD_DIM], q) for st in starts]
        s = [jnp.where(tri, s[count], s[0])] + s[1:count]
        s = [x * (SCALE * LOG2E) + bias[i] for i, x in enumerate(s)]
        top = functools.reduce(jnp.maximum, s)
        top = jnp.max(top, axis=0, keepdims=True)
        p = [jnp.exp2(x - top) for x in s]
        total = jnp.sum(functools.reduce(jnp.add, p), axis=0, keepdims=True)
        low = [x.astype(BF) for x in p]
        zero = jnp.zeros_like(low[0])
        low = [jnp.where(tri, zero, low[0])] + low[1:] + [jnp.where(tri, low[0], zero)]
        acc = None
        for i in range(count + 1):
            d = dot_nn(vt[:, pl.ds(starts[i], rows)], low[i])
            acc = d if acc is None else acc + d
        out_ref[:, h * HEAD_DIM : (h + 1) * HEAD_DIM] = (acc / total).T.astype(BF)
        lse_ref[h : h + 1, :] = top + jnp.log2(total)


def attend_backward(
    blocks_ref, q_ref, prev_ref, own_ref, qseg_ref, kseg_ref, dout_ref, lse_ref, dq_ref, dboth_ref, both, kt, bias, dkv
):
    count, rows, heads = bias.shape[0], q_ref.shape[0], q_ref.shape[1] // HEAD_DIM
    r = pl.program_id(0)
    a = blocks_ref[r]

    @pl.when(r == 0)
    def _():
        in_order(blocks_ref, prev_ref, own_ref, both, count, rows)
        for i in range(2 * count):
            kt[:, i * rows : (i + 1) * rows] = both[i * rows : (i + 1) * rows, :HEAD_DIM].T
        dkv[...] = jnp.zeros_like(dkv)

    tri = lax.broadcasted_iota(jnp.int32, (rows, rows), 0) <= lax.broadcasted_iota(jnp.int32, (rows, rows), 1)
    fill_bias(a, rows, count, qseg_ref, kseg_ref, bias, tri)
    starts = [pl.multiple_of((a + i) * rows, rows) for i in range(count + 1)]
    for h in range(heads):
        cols = slice(h * HEAD_DIM, (h + 1) * HEAD_DIM)
        q, dout = q_ref[:, cols], dout_ref[:, cols]
        lse = lse_ref[h : h + 1, :]
        s = [dot_nt(both[pl.ds(st, rows), :HEAD_DIM], q) for st in starts]
        dp = [dot_nt(both[pl.ds(st, rows), HEAD_DIM:], dout) for st in starts]
        s = [jnp.where(tri, s[count], s[0])] + s[1:count]
        dp = [jnp.where(tri, dp[count], dp[0])] + dp[1:count]
        p = [jnp.exp2(x * (SCALE * LOG2E) + bias[i] - lse) for i, x in enumerate(s)]
        inner = functools.reduce(jnp.add, [x * y for x, y in zip(p, dp)])
        inner = jnp.sum(inner, axis=0, keepdims=True)
        ds = [(x * (y - inner)).astype(BF) for x, y in zip(p, dp)]
        low = [x.astype(BF) for x in p]
        zero = jnp.zeros_like(low[0])
        low = [jnp.where(tri, zero, low[0])] + low[1:] + [jnp.where(tri, low[0], zero)]
        ds = [jnp.where(tri, zero, ds[0])] + ds[1:] + [jnp.where(tri, ds[0], zero)]
        acc = None
        for i in range(count + 1):
            d = dot_nn(kt[:, pl.ds(starts[i], rows)], ds[i])
            acc = d if acc is None else acc + d
            dkv[pl.ds(starts[i], rows), :HEAD_DIM] += dot_nn(ds[i], q)
            dkv[pl.ds(starts[i], rows), HEAD_DIM:] += dot_nn(low[i], dout)
        dq_ref[:, cols] = (acc * SCALE).T.astype(BF)

    @pl.when(r == count - 1)
    def _():
        for j in range(count):
            at = blocks_ref[j] * rows
            for k in range(2):
                blk = dkv[pl.ds(at + k * count * rows, rows), :]
                first = k * 2 * HEAD_DIM
                dboth_ref[j * rows : (j + 1) * rows, first : first + HEAD_DIM] = (blk[:, :HEAD_DIM] * SCALE).astype(BF)
                dboth_ref[j * rows : (j + 1) * rows, first + HEAD_DIM : first + 2 * HEAD_DIM] = blk[:, HEAD_DIM:].astype(BF)


def whole_spec(shape):
    return pl.BlockSpec(shape, lambda r, b: (0,) * len(shape))


def attention_forward(blocks, queries, prev, own, qseg, kseg, count):
    total, width = queries.shape
    rows = total // count
    heads = width // HEAD_DIM
    return pl.pallas_call(
        attend_forward,
        grid_spec=pltpu.PrefetchScalarGridSpec(
            num_scalar_prefetch=1,
            grid=(count,),
            in_specs=[
                pl.BlockSpec((rows, width), lambda r, b: (r, 0)),
                whole_spec(prev.shape),
                whole_spec(own.shape),
                pl.BlockSpec((1, rows), lambda r, b: (0, b[r])),
                whole_spec(kseg.shape),
            ],
            out_specs=[
                pl.BlockSpec((rows, width), lambda r, b: (r, 0)),
                pl.BlockSpec((heads, rows), lambda r, b: (0, r)),
            ],
            scratch_shapes=[
                pltpu.VMEM((2 * total, 2 * HEAD_DIM), BF),
                pltpu.VMEM((HEAD_DIM, 2 * total), BF),
                pltpu.VMEM((count, rows, rows), F32),
            ],
        ),
        out_shape=[jax.ShapeDtypeStruct((total, width), BF), jax.ShapeDtypeStruct((heads, total), F32)],
        compiler_params=pltpu.CompilerParams(vmem_limit_bytes=40 << 20),
        cost_estimate=pl.CostEstimate(flops=1, bytes_accessed=1, transcendentals=0),
        name="attend_forward",
    )(blocks, queries, prev, own, qseg, kseg)


def attention_backward(blocks, queries, prev, own, qseg, kseg, dout, lse, count):
    total, width = queries.shape
    rows = total // count
    heads = width // HEAD_DIM
    return pl.pallas_call(
        attend_backward,
        grid_spec=pltpu.PrefetchScalarGridSpec(
            num_scalar_prefetch=1,
            grid=(count,),
            in_specs=[
                pl.BlockSpec((rows, width), lambda r, b: (r, 0)),
                whole_spec(prev.shape),
                whole_spec(own.shape),
                pl.BlockSpec((1, rows), lambda r, b: (0, b[r])),
                whole_spec(kseg.shape),
                pl.BlockSpec((rows, width), lambda r, b: (r, 0)),
                pl.BlockSpec((heads, rows), lambda r, b: (0, r)),
            ],
            out_specs=[
                pl.BlockSpec((rows, width), lambda r, b: (r, 0)),
                whole_spec((total, 4 * HEAD_DIM)),
            ],
            scratch_shapes=[
                pltpu.VMEM((2 * total, 2 * HEAD_DIM), BF),
                pltpu.VMEM((HEAD_DIM, 2 * total), BF),
                pltpu.VMEM((count, rows, rows), F32),
                pltpu.VMEM((2 * total, 2 * HEAD_DIM), F32),
            ],
        ),
        out_shape=[
            jax.ShapeDtypeStruct((total, width), BF),
            jax.ShapeDtypeStruct((total, 4 * HEAD_DIM), BF),
        ],
        compiler_params=pltpu.CompilerParams(vmem_limit_bytes=40 << 20),
        cost_estimate=pl.CostEstimate(flops=1, bytes_accessed=1, transcendentals=0),
        name="attend_backward",
    )(blocks, queries, prev, own, qseg, kseg, dout, lse)


def gelu_parts(g):
    root = 0.7978845608028654
    inner = jnp.tanh(root * (g + 0.044715 * (g * g * g)))
    half = 0.5 * (1.0 + inner)
    slope = half + 0.5 * g * (1.0 - inner * inner) * (root * (1.0 + 3 * 0.044715 * (g * g)))
    return g * half, slope


def ffn_forward_kernel(nx, *refs):
    xs, cs, (gate, up) = refs[:nx], refs[nx : 2 * nx], refs[2 * nx : 2 * nx + 2]
    hid, act, pg, x_out, c_out, x_all, c_all, sems, o_sems = refs[2 * nx + 2 :]
    rows, n = xs[0].shape[0], gate.shape[1]
    i = pl.program_id(0)
    x_in = [pltpu.make_async_copy(x, x_all.at[pl.ds(j * rows, rows)], sems.at[j]) for j, x in enumerate(xs)]
    c_in = [pltpu.make_async_copy(x, c_all.at[pl.ds(j * rows, rows)], sems.at[nx + j]) for j, x in enumerate(cs)]
    outs = [pltpu.make_async_copy(src, dst, o_sems.at[j]) for j, (src, dst) in enumerate(((x_all, x_out), (c_all, c_out)))]

    @pl.when(i == 0)
    def _():
        for copy in x_in + c_in:
            copy.start()
        for copy in x_in:
            copy.wait()
        outs[0].start()

    @pl.when(i == 1)
    def _():
        for copy in c_in:
            copy.wait()
        outs[1].start()

    x = x_all[pl.ds(pl.multiple_of(i * rows, rows), rows), :]
    step = n // 3 if n % 384 == 0 else n
    for j in range(0, n, step):
        g = dot_nn(x, gate[:, j : j + step])
        u = dot_nn(x, up[:, j : j + step])
        value, slope = gelu_parts(g)
        hid[:, j : j + step] = (value * u).astype(BF)
        act[:, j : j + step] = value.astype(BF)
        pg[:, j : j + step] = (slope * u).astype(BF)

    @pl.when(i == pl.num_programs(0) - 1)
    def _():
        for o in outs:
            o.wait()


def ffn_forward(x_blocks, c_blocks, both):
    rows, width = x_blocks[0].shape
    count, n = len(x_blocks), both.shape[1] // 3
    total = count * rows
    anywhere = pl.BlockSpec(memory_space=pl.ANY)
    block = pl.BlockSpec((rows, n), lambda i: (i, 0))
    kept = jax.ShapeDtypeStruct((total, n), BF)
    return pl.pallas_call(
        functools.partial(ffn_forward_kernel, count),
        grid=(count,),
        in_specs=[anywhere] * (2 * count) + [pl.BlockSpec((width, n), lambda i: (0, 0)), pl.BlockSpec((width, n), lambda i: (0, 1))],
        out_specs=[block] * 3 + [anywhere] * 2,
        scratch_shapes=[
            pltpu.VMEM((total, width), BF),
            pltpu.VMEM((total, width), BF),
            pltpu.SemaphoreType.DMA((2 * count,)),
            pltpu.SemaphoreType.DMA((2,)),
        ],
        out_shape=[kept] * 3 + [jax.ShapeDtypeStruct((total, width), BF)] * 2,
        compiler_params=pltpu.CompilerParams(vmem_limit_bytes=48 << 20),
        cost_estimate=pl.CostEstimate(flops=4 * total * width * n, bytes_accessed=20 << 20, transcendentals=total * n),
        name="ffn_forward",
    )(*x_blocks, *c_blocks, both, both)


def ffn_backward_kernel(cot, act, pg, down, grads):
    n = down.shape[1]
    x = cot[...]
    step = n // 3 if n % 384 == 0 else n
    for j in range(0, n, step):
        d = dot_nn(x, down[:, j : j + step])
        grads[:, j : j + step] = (d * pg[:, j : j + step].astype(F32)).astype(BF)
        grads[:, n + j : n + j + step] = (d * act[:, j : j + step].astype(F32)).astype(BF)


def ffn_backward(cot, act, pg, down, count):
    total, width = cot.shape
    n = down.shape[1] // 3
    rows = total // count
    block = pl.BlockSpec((rows, n), lambda i: (i, 0))
    return pl.pallas_call(
        ffn_backward_kernel,
        grid=(count,),
        in_specs=[pl.BlockSpec((rows, width), lambda i: (i, 0)), block, block, pl.BlockSpec((width, n), lambda i: (0, 2))],
        out_specs=pl.BlockSpec((rows, 2 * n), lambda i: (i, 0)),
        out_shape=jax.ShapeDtypeStruct((total, 2 * n), BF),
        compiler_params=pltpu.CompilerParams(vmem_limit_bytes=40 << 20),
        cost_estimate=pl.CostEstimate(flops=2 * total * width * n, bytes_accessed=16 << 20, transcendentals=0),
        name="ffn_backward",
    )(cot, act, pg, down)


def rms_inverse(values):
    return lax.rsqrt(jnp.mean(values * values, axis=-1, keepdims=True) + EPSILON)


def norm_backward(grad_normed, values, inv_rms, gain_row):
    scaled = grad_normed * gain_row
    inner_sum = jnp.mean(scaled * values, axis=-1, keepdims=True)
    return inv_rms * scaled - values * (inv_rms * inv_rms * inv_rms) * inner_sum


def mm(a, b):
    return dot_nn(a, b)


def mm_tn(a, b):
    return lax.dot_general(a, b, (((0,), (0,)), ((), ())), preferred_element_type=F32)


def local(tokens, cotangent, segment_ids, w_query, w_keyval, w_out, w_gate, w_up, w_down, norm_gains):
    nt = lax.axis_size("tensor")
    t, c = lax.axis_index("tensor"), lax.axis_index("context")
    tokens, cotangent = tokens[0], cotangent[0]
    own_rows, width = tokens.shape
    rows = own_rows * nt
    if rows != WINDOW:
        raise ValueError("shard length")
    order = tensor_order(nt)
    blocks = jnp.array(order, jnp.int32) ^ t

    part = w_keyval.shape[0]
    kv_cols = w_keyval.shape[1]
    nf, nc = lax.axis_size("fsdp"), lax.axis_size("context")
    small_own = jnp.concatenate([w_keyval, norm_gains.T, jnp.zeros((part, 126), BF)], axis=1)
    first_own = jnp.concatenate([w_query, small_own], axis=0)
    wo_own, wd_own = w_out.T, w_down.T
    slots = slots_of()
    both = ("fsdp", "context")

    first_along = along(first_own)
    first_early = across(first_own)
    token_blocks = tensor_blocks(tokens)
    first_along = along(first_own)
    first_early = across(first_own)
    token_blocks = tensor_blocks(tokens)
    wg = lax.all_gather(w_gate, both, axis=0, tiled=True)
    first_along = jnp.stack(first_along)
    first_across = across(first_along, first_early)
    gate_up = jnp.concatenate([w_gate, w_up, wd_own], axis=1)
    gate_up = lax.all_gather(after(gate_up, *first_along), both, axis=0, tiled=True)
    first_along = jnp.stack(first_along)
    first_across = across(first_along, first_early)
    wu = lax.all_gather(after(w_up, *first_across), both, axis=0, tiled=True)
    wo_along = along(wo_own, first_along)
    wo_all = jnp.stack([wo_own, *wo_along])
    wo_across = across(wo_all, first_across)

    own_rows_q = nt * part
    wq, small = place(slots, gathered(first_own, first_along, first_early, first_across), [(0, own_rows_q), (own_rows_q, own_rows_q + part)])
    small_blocks = tensor_blocks(small.reshape(nf * nc, part, -1))
    cot_blocks = tensor_blocks(cotangent, small_blocks)
    small = jnp.zeros((nf * nc, nt, part, small.shape[1]), BF)
    for i in range(nt):
        small = lax.dynamic_update_index_in_dim(small, small_blocks[i], t ^ order[i], 1)
    small = small.reshape(width, -1)
    wkv = small[:, :kv_cols]
    gain_cols = small[:, kv_cols : kv_cols + 2].astype(F32)
    gains = gain_cols.T
    gain_one, gain_two = gains[0:1], gains[1:2]

    ids = segment_ids[0]
    own_seg = lax.dynamic_slice_in_dim(ids, c * rows, rows, 0)
    prev_seg = lax.dynamic_slice_in_dim(ids, jnp.maximum(c - 1, 0) * rows, rows, 0)
    prev_seg = jnp.where(c > 0, prev_seg, -1)
    qseg = own_seg[None, :]
    kseg = jnp.broadcast_to(jnp.concatenate([prev_seg, own_seg])[:, None], (2 * rows, 128))

    xin = jnp.concatenate(token_blocks, axis=0).astype(F32)
    inv_one_rows = rms_inverse(xin)
    normed_one = (xin * inv_one_rows * gain_one).astype(BF)
    keyvals = mm(normed_one, wkv).astype(BF)
    earlier = shift(keyvals, "context", 1)
    queries = mm(normed_one, wq).astype(BF)
    heads_out, lse = attention_forward(blocks, after(queries, cot_blocks[1]), earlier, keyvals, qseg, kseg, nt)
    (wo_t,) = place(slots, [wo_all] + behind(wo_across, heads_out))
    heads_now = heads_out
    branch = reduce_tensor(lambda i, j: dot_nt(heads_now[i:j], wo_t), rows)
    own_in = tokens.astype(F32)
    middle = own_in + branch
    inv_two = rms_inverse(middle)
    normed_two = (middle * inv_two * gain_two).astype(BF)
    second_blocks = tensor_blocks(normed_two)

    hidden, act, pg, second_rows, cot_rows = ffn_forward(second_blocks, cot_blocks, gate_up)
    part_down = slabs_of(mm_tn(cot_rows, hidden).astype(BF))
    got_down = half_sent(part_down)
    grads = ffn_backward(after(cot_rows, part_down), act, pg, gate_up, nt)
    ff = w_gate.shape[1]
    gate_up, wd_t = gate_up[:, : 2 * ff], gate_up[:, 2 * ff :]
    half = rows // 2
    two_away = dot_nt(grads[half:], gate_up).astype(BF)
    two_own = dot_nt(grads[:half], gate_up)
    d_two = reduce_halves(two_away, two_own)
    part_gate = slabs_of(mm_tn(after(second_rows, two_away, two_own), grads[:, :ff]).astype(BF))
    got_down = behind(got_down, part_gate)
    grad_down = rest_large(half_sum(part_down, got_down))
    got_gate = half_sent(part_gate, got_down)
    part_up = slabs_of(mm_tn(after(second_rows, part_gate), grads[:, ff:]).astype(BF))

    gain_two_part = jnp.sum(d_two * middle * inv_two, axis=0, keepdims=True)
    d_middle = cotangent.astype(F32) + norm_backward(d_two, middle, inv_two, gain_two)
    back_blocks = tensor_blocks(d_middle.astype(BF))
    hidden = after(hidden, back_blocks[1])
    ffn = reduce_tensor(lambda i, j: dot_nt(hidden[i:j], wd_t), rows)
    output = (middle + ffn).astype(BF)
    back_rows = jnp.concatenate(back_blocks, axis=0)
    got_gate = behind(got_gate, part_up)
    grad_gate = rest_large(half_sum(part_gate, got_gate))
    got_up = half_sent(part_up, got_gate)
    d_head = mm(after(back_rows, *got_gate), wo_t).astype(BF)
    dq, dboth = attention_backward(blocks, queries, earlier, keyvals, qseg, kseg, d_head, lse, nt)
    dboth = reduce_halves(dboth[rows // 2 :], dboth[: rows // 2].astype(F32))
    later = shift(dboth[:, :kv_cols].astype(BF), "context", -1)
    dkv = (dboth[:, kv_cols:] + later.astype(F32)).astype(BF)
    got_up = behind(got_up, dq)
    part_out = slabs_of(mm_tn(after(back_rows, dq), heads_out).astype(BF))

    d_one = reduce_tensor(lambda i, j: dot_nt(dq[i:j], wq), rows) + dot_nt(dkv, wkv)
    inv_one = rms_inverse(own_in)
    input_grad = d_middle + norm_backward(d_one, own_in, inv_one, gain_one)

    query_part = mm_tn(normed_one, dq)
    kv_part = mm_tn(normed_one[:own_rows], dkv)
    gain_one_part = jnp.sum(query_part * wq.astype(F32), axis=1, keepdims=True) + jnp.sum(kv_part * wkv.astype(F32), axis=1, keepdims=True)
    gain_one_part = gain_one_part / gain_cols[:, 0:1]
    small_part = jnp.concatenate([kv_part, gain_one_part, gain_two_part.T, jnp.zeros((width, 126), F32)], axis=1)
    small_part = small_part.reshape(-1, nt, part, kv_cols + 128)
    small_part = jnp.stack([lax.dynamic_index_in_dim(small_part, t ^ k, 1, False) for k in order])
    small_part = after(small_part, *got_up)
    small_part = reduce_tensor(lambda i, j: small_part[i:j], nt)[0].astype(BF)
    last = jnp.concatenate([slabs_of(query_part.astype(BF)), part_out], axis=2)
    got_last = half_sent(last, got_up)
    grad_up = rest_large(half_sum(part_up, got_up))
    small_part = small_part.reshape(nf, nc, part, kv_cols + 128)
    got_small = half_sent(small_part)
    small_sum, back = rest_small(half_sum(small_part, got_small))
    last, _ = rest_small(half_sum(last, got_last), back)
    grad_query, grad_out = last[: nt * part], last[nt * part :]
    grad_keyval = small_sum[:, :kv_cols]
    grad_gains = small_sum[:, kv_cols : kv_cols + 2].T
    return (output[None], input_grad[None], grad_query, grad_keyval, grad_out.T, grad_gate, grad_up, grad_down.T, grad_gains)


def solution(mesh):
    rows = P("fsdp", ("context", "tensor"), None)
    column = P(("fsdp", "context"), "tensor")
    row = P("tensor", ("fsdp", "context"))
    small = P(("fsdp", "context", "tensor"), None)
    gains = P(None, ("fsdp", "context", "tensor"))
    return jax.shard_map(
        local,
        mesh=mesh,
        in_specs=(rows, rows, P("fsdp", None), column, small, row, column, column, row, gains),
        out_specs=(rows, rows, column, small, row, column, column, row, gains),
        check_vma=False,
    )
```

profile of v0, /device:TPU:0, one launch (start us, length us, event | category | flops | bytes accessed | tf_op | source)
XLA Modules:
  0.0 447.6 jit_solution(13374882857163956515)
XLA Ops:
  9.7 3.0 collective-permute-start.3
  12.8 2.6 collective-permute-start.4
  15.4 2.6 pad_maximum_fusion.3
  18.0 2.5 collective-permute-done.3
  20.5 8.7 %collective-permute-done.4 = bf16[240,384]{1,0:T(8,128)(2,1)S(1)} collective-permute-done((bf16[240,384]{1,0:T(8,128)(2,1)S(1)}, bf16[240,384]{1,0:T(8,128)(2,1)S(1)}, u32[]{:S(2)}, u32[]{:S(2)}) %collective-permute-start.4) | collective-permute-done | bytes 184352 | tf_op jit(solution)/shard_map/ppermute | solution.py:21
  32.4 3.6 collective-permute-done.6
  42.5 13.4 %collective-permute-done.7.refs_3_ = bf16[3,240,384]{2,1,0:T(8,128)(2,1)S(1)} collective-permute-done((bf16[3,240,384]{2,1,0:T(8,128)(2,1)S(1)}, bf16[3,240,384]{2,1,0:T(8,128)(2,1)S(1)}, u32[]{:S(2)}, u32[]{:S(2)}) %collective-permute-start.7) | collective-permute-done | bytes 552992 | tf_op jit(solution)/shard_map/ppermute | solution.py:21
  56.6 3.3 place.2
  62.5 2.5 collective-permute-start.16
  65.4 3.5 collective-permute-done.8
  73.6 2.3 fusion
  76.0 5.3 %fusion.2 = bf16[1024,1536]{1,0:T(8,128)(2,1)S(1)} fusion(f32[1536]{0:T(1024)S(1)} %get-tuple-element.106, f32[1024]{0:T(1024)S(1)} %add_rsqrt_fusion, bf16[256,1536]{1,0:T(8,128)(2,1)S(1)} %collective-permute-done.2, bf16[256,1536]{1,0:T(8,128)(2,1)} %collective-permute-done.1, bf16[256,1536]{1,0:T(8,128)(2,1)S(1)} %collective-permute-done, ...), kind=kLoop, calls=%fused_computation.7 | loop fusion | flops 17301504 | bytes 6301696 | tf_op jit(solution)/shard_map/convert_element_type | solution.py:534
  82.4 4.5 %collective-permute-start.12 = (bf16[1024,256]{1,0:T(8,128)(2,1)S(1)}, bf16[1024,256]{1,0:T(8,128)(2,1)S(1)}, u32[]{:S(2)}, u32[]{:S(2)}) collective-permute-start(bf16[1024,256]{1,0:T(8,128)(2,1)S(1)} %convolution_convert_fusion.8.own_ref), channel_id=1, source_target_pairs={{0,4},{1,5},{2,6},{3,7},{8,12},{9,13},{10,14},{11,15},{16,20},{17,... | collective-permute-start | bytes 1572872 | tf_op jit(solution)/shard_map/ppermute | solution.py:27
  90.2 7.9 %collective-permute-done.12.prev_ref = bf16[1024,256]{1,0:T(8,128)(2,1)S(1)} collective-permute-done((bf16[1024,256]{1,0:T(8,128)(2,1)S(1)}, bf16[1024,256]{1,0:T(8,128)(2,1)S(1)}, u32[]{:S(2)}, u32[]{:S(2)}) %collective-permute-start.12) | collective-permute-done | bytes 524320 | tf_op jit(solution)/shard_map/ppermute | solution.py:27
  98.4 9.4 %attend_forward.1 = (bf16[1024,384]{1,0:T(8,128)(2,1)S(1)}, f32[3,1024]{1,0:T(4,128)S(1)}) custom-call(s32[4]{0:T(128)S(1)} %broadcast_xor_fusion.blocks_ref, bf16[1024,384]{1,0:T(8,128)(2,1)S(1)} %convolution_convert_fusion.7.q_ref, bf16[1024,256]{1,0:T(8,128)(2,1)S(1)} %collective-permute-done.12.prev_ref, ...), custom_call_target="tpu_custom_call" | custom-call | flops 1 | bytes 1 | tf_op jit(solution)/shard_map/attend_forward/pallas_call | solution.py:289
  108.7 3.1 place.3
  111.9 2.4 convolution_convert_fusion.4
  114.3 3.4 collective-permute-done.17
  119.7 18.9 %collective-permute-done.18 = bf16[256,1536]{1,0:T(8,128)(2,1)S(1)} collective-permute-done((bf16[256,1536]{1,0:T(8,128)(2,1)S(1)}, bf16[256,1536]{1,0:T(8,128)(2,1)S(1)}, u32[]{:S(2)}, u32[]{:S(2)}) %collective-permute-start.18) | collective-permute-done | bytes 786464 | tf_op jit(solution)/shard_map/ppermute | solution.py:21
  140.4 17.7 %collective-permute-done.19.refs_1_ = bf16[256,1536]{1,0:T(8,128)(2,1)} collective-permute-done((bf16[256,1536]{1,0:T(8,128)(2,1)S(1)}, bf16[256,1536]{1,0:T(8,128)(2,1)}, u32[]{:S(2)}, u32[]{:S(2)}) %collective-permute-start.19) | collective-permute-done | bytes 786464 | tf_op jit(solution)/shard_map/ppermute | solution.py:21
  158.2 2.6 collective-permute-done.21.refs_3_
  160.8 31.6 %all-gather.2.cloned.1.call-done.refs_8_.refs_9_.down = bf16[1536,3456]{1,0:T(8,128)(2,1)} async-done(((bf16[192,3456]{1,0:T(8,128)(2,1)}), bf16[1536,3456]{1,0:T(8,128)(2,1)}) %all-gather.2.cloned.1.call-update) | async-done | bytes 10616848 | tf_op jit(solution)/shard_map/all_gather | solution.py:504
  192.4 17.0 %ffn_forward.1 = (bf16[1024,1152]{1,0:T(8,128)(2,1)}, bf16[1024,1152]{1,0:T(8,128)(2,1)}, bf16[1024,1152]{1,0:T(8,128)(2,1)}, bf16[1024,1536]{1,0:T(8,128)(2,1)}, bf16[1024,1536]{1,0:T(8,128)(2,1)}) custom-call(bf16[256,1536]{1,0:T(8,128)(2,1)S(1)} %multiply_convert_fusion.refs_0_, bf16[256,1536]{1,0:T(8,128)(2,1)} %collective-permute-done.19.refs_1_, ...), custom_call_target="tpu_custom_call" | custom-call | flops 7247757312 | bytes 20971520 | tf_op jit(solution)/shard_map/ffn_forward/pallas_call | solution.py:411
  209.4 7.0 %convolution_convert_fusion.2 = bf16[1536,1152]{1,0:T(8,128)(2,1)S(1)} fusion(bf16[1024,1536]{1,0:T(8,128)(2,1)} %get-tuple-element.58.cot, bf16[1024,1152]{1,0:T(8,128)(2,1)} %get-tuple-element.61), kind=kOutput, calls=%fused_computation.4 | convolution fusion | flops 3625648128 | bytes 9043968 | tf_op jit(solution)/shard_map/dot_general | solution.py:471
  220.3 8.0 %ffn_backward.1 = bf16[1024,2304]{1,0:T(8,128)(2,1)S(1)} custom-call(bf16[1024,1536]{1,0:T(8,128)(2,1)S(1)} %copy-done.1, bf16[1024,1152]{1,0:T(8,128)(2,1)S(1)} %copy-done.3, bf16[1024,1152]{1,0:T(8,128)(2,1)S(1)} %copy-done.4, bf16[1536,3456]{1,0:T(8,128)(2,1)} %all-gather.2.cloned.1.call-done.refs_8_.refs_9_.down), custom_call_target="tpu_custom_call" | custom-call | flops 3623878656 | bytes 16777216 | tf_op jit(solution)/shard_map/ffn_backward/pallas_call | solution.py:444
  228.4 8.6 %fusion.16 = bf16[512,1536]{1,0:T(8,128)(2,1)S(1)} fusion(bf16[1536,3456]{1,0:T(8,128)(2,1)} %all-gather.2.cloned.1.call-done.refs_8_.refs_9_.down, bf16[1024,2304]{1,0:T(8,128)(2,1)S(1)} %ffn_backward.1), kind=kOutput, calls=%fused_computation.28 | convolution fusion | flops 3624665088 | bytes 11010048 | tf_op jit(solution)/shard_map/dot_general | solution.py:167
  237.1 3.8 fusion.5
  241.0 8.5 %convolution_convert_fusion.1 = bf16[1536,1152]{1,0:T(8,128)(2,1)} fusion(bf16[1024,1536]{1,0:T(8,128)(2,1)} %get-tuple-element.66, bf16[1024,2304]{1,0:T(8,128)(2,1)S(1)} %ffn_backward.1), kind=kOutput, calls=%fused_computation.3 | convolution fusion | flops 3625648128 | bytes 9043968 | tf_op jit(solution)/shard_map/dot_general | solution.py:471
  254.0 4.2 collective-permute-done.31
  258.1 3.2 fusion.7
  261.8 7.1 %convolution_convert_fusion = bf16[1536,1152]{1,0:T(8,128)(2,1)S(1)} fusion(bf16[1024,1536]{1,0:T(8,128)(2,1)} %get-tuple-element.66, bf16[1024,2304]{1,0:T(8,128)(2,1)} %copy-done), kind=kOutput, calls=%fused_computation.2 | convolution fusion | flops 3625648128 | bytes 9043968 | tf_op jit(solution)/shard_map/dot_general | solution.py:471
  279.5 15.4 %collective-permute-done.26 = bf16[256,1536]{1,0:T(8,128)(2,1)} collective-permute-done((bf16[256,1536]{1,0:T(8,128)(2,1)}, bf16[256,1536]{1,0:T(8,128)(2,1)}, u32[]{:S(2)}, u32[]{:S(2)}) %collective-permute-start.26) | collective-permute-done | bytes 786464 | tf_op jit(solution)/shard_map/ppermute | solution.py:21
  294.9 5.8 %fusion.13 = bf16[512,1536]{1,0:T(8,128)(2,1)} fusion(bf16[1536,3456]{1,0:T(8,128)(2,1)} %all-gather.2.cloned.1.call-done.refs_8_.refs_9_.down, bf16[1024,1152]{1,0:T(8,128)(2,1)} %get-tuple-element.61), kind=kOutput, calls=%fused_computation.27 | convolution fusion | flops 1812725760 | bytes 6291456 | tf_op jit(solution)/shard_map/dot_general | solution.py:167
  301.2 10.6 %collective-permute-done.32 = bf16[4,192,1152]{2,1,0:T(8,128)(2,1)} collective-permute-done((bf16[4,192,1152]{2,1,0:T(8,128)(2,1)}, bf16[4,192,1152]{2,1,0:T(8,128)(2,1)}, u32[]{:S(2)}, u32[]{:S(2)}) %collective-permute-start.32) | collective-permute-done | bytes 1769504 | tf_op jit(solution)/shard_map/ppermute | solution.py:21
  312.3 3.1 fusion.9
  319.6 15.2 %attend_backward.1 = (bf16[1024,384]{1,0:T(8,128)(2,1)S(1)}, bf16[1024,512]{1,0:T(8,128)(2,1)S(1)}) custom-call(s32[4]{0:T(128)S(1)} %broadcast_xor_fusion.blocks_ref, bf16[1024,384]{1,0:T(8,128)(2,1)S(1)} %convolution_convert_fusion.7.q_ref, bf16[1024,256]{1,0:T(8,128)(2,1)S(1)} %copy-done.8, bf16[1024,256]{1,0:T(8,128)(2,1)S(1)} %copy-done.6, ...), custom_call_target="tpu_custom_call" | custom-call | flops 1 | bytes 1 | tf_op jit(solution)/shard_map/attend_backward/pallas_call | solution.py:322
  344.4 3.7 collective-permute-done.36
  349.9 4.7 %convolution_add_fusion.2 = f32[512,1536]{1,0:T(8,128)S(1)} fusion(bf16[512,1536]{1,0:T(8,128)(2,1)} %collective-permute-done.27, bf16[1536,3456]{1,0:T(8,128)(2,1)} %all-gather.2.cloned.1.call-done.refs_8_.refs_9_.down, bf16[1024,1152]{1,0:T(8,128)(2,1)S(1)} %copy-done.56), kind=kOutput, calls=%fused_computation.20 | convolution fusion | flops 1813512192 | bytes 9437184 | tf_op jit(solution)/shard_map/dot_general | solution.py:167
  361.1 2.7 collective-permute-start.39
  363.7 3.2 fusion.8
  369.0 2.9 convolution_add_fusion
  377.1 21.1 %collective-permute-done.41 = bf16[1,8,48,384]{3,2,1,0:T(8,128)(2,1)S(1)} collective-permute-done((bf16[1,8,48,384]{3,2,1,0:T(8,128)(2,1)S(1)}, bf16[1,8,48,384]{3,2,1,0:T(8,128)(2,1)S(1)}, u32[]{:S(2)}, u32[]{:S(2)}) %collective-permute-start.41) | collective-permute-done | bytes 294944 | tf_op jit(solution)/shard_map/ppermute | solution.py:21
  398.3 2.4 collective-permute-start.42
  404.3 3.1 collective-permute-start.44
  410.9 2.6 collective-permute-done.45
  414.7 3.1 collective-permute-start.48
  420.5 4.5 %collective-permute-done.46 = bf16[384,384]{1,0:T(8,128)(2,1)S(1)} collective-permute-done((bf16[384,384]{1,0:T(8,128)(2,1)}, bf16[384,384]{1,0:T(8,128)(2,1)S(1)}, u32[]{:S(2)}, u32[]{:S(2)}) %collective-permute-start.46) | collective-permute-done | bytes 294944 | tf_op jit(solution)/shard_map/ppermute | solution.py:21
  425.0 10.9 %collective-permute-done.47 = bf16[384,384]{1,0:T(8,128)(2,1)S(1)} collective-permute-done((bf16[384,384]{1,0:T(8,128)(2,1)}, bf16[384,384]{1,0:T(8,128)(2,1)S(1)}, u32[]{:S(2)}, u32[]{:S(2)}) %collective-permute-start.47) | collective-permute-done | bytes 294944 | tf_op jit(solution)/shard_map/ppermute | solution.py:21
  (284 shorter events, 95.1 us)
Async XLA Ops:
  7.2 185.2 %all-gather.2.cloned.1.call-start = ((), (), s32[]{:S(2)}) async-start(), calls=%async_computation.3 | async-start | bytes 11943936 | tf_op jit(solution)/shard_map/all_gather | solution.py:504
  9.7 10.7 %collective-permute-start.3 = (bf16[240,384]{1,0:T(8,128)(2,1)S(1)}, bf16[240,384]{1,0:T(8,128)(2,1)S(1)}, u32[]{:S(2)}, u32[]{:S(2)}) collective-permute-start(bf16[240,384]{1,0:T(8,128)(2,1)S(1)} %get-tuple-element.128), channel_id=1, source_target_pairs={{0,8},{8,0},{16,24},{24,16},{1,9},{9,1},{17,25},{25,17},{2,10},{10... | collective-permute-start | bytes 552968 | tf_op jit(solution)/shard_map/ppermute | solution.py:21
  12.8 16.4 %collective-permute-start.4 = (bf16[240,384]{1,0:T(8,128)(2,1)S(1)}, bf16[240,384]{1,0:T(8,128)(2,1)S(1)}, u32[]{:S(2)}, u32[]{:S(2)}) collective-permute-start(bf16[240,384]{1,0:T(8,128)(2,1)S(1)} %get-tuple-element.128), channel_id=1, source_target_pairs={{0,16},{8,24},{16,0},{24,8},{1,17},{9,25},{17,1},{25,9},{2,18},{10... | collective-permute-start | bytes 552968 | tf_op jit(solution)/shard_map/ppermute | solution.py:21
  15.4 13.8 %collective-permute-start.5 = (bf16[240,384]{1,0:T(8,128)(2,1)S(1)}, bf16[240,384]{1,0:T(8,128)(2,1)S(1)}, u32[]{:S(2)}, u32[]{:S(2)}) collective-permute-start(bf16[240,384]{1,0:T(8,128)(2,1)S(1)} %get-tuple-element.128), channel_id=1, source_target_pairs={{0,24},{8,16},{16,8},{24,0},{1,25},{9,17},{17,9},{25,1},{2,26},{10... | collective-permute-start | bytes 552968 | tf_op jit(solution)/shard_map/ppermute | solution.py:21
  29.2 337.8 %reduce-scatter.8.cloned.1.call-start = ((), (), s32[]{:S(2)}) async-start(), calls=%async_computation.6 | async-start | bytes 2211840 | tf_op jit(solution)/shard_map/reduce_scatter | solution.py:151
  29.2 6.8 %collective-permute-start.6 = (bf16[240,384]{1,0:T(8,128)(2,1)S(1)}, bf16[240,384]{1,0:T(8,128)(2,1)S(1)}, u32[]{:S(2)}, u32[]{:S(2)}) collective-permute-start(bf16[240,384]{1,0:T(8,128)(2,1)S(1)} %get-tuple-element.128), channel_id=1, source_target_pairs={{0,4},{4,0},{1,5},{5,1},{2,6},{6,2},{3,7},{7,3},{8,12},{12,8},{9,1... | collective-permute-start | bytes 552968 | tf_op jit(solution)/shard_map/ppermute | solution.py:21
  30.8 34.4 %collective-permute-start = (bf16[256,1536]{1,0:T(8,128)(2,1)S(1)}, bf16[256,1536]{1,0:T(8,128)(2,1)S(1)}, u32[]{:S(2)}, u32[]{:S(2)}) collective-permute-start(bf16[256,1536]{1,0:T(8,128)(2,1)S(1)} %bitcast.154), channel_id=1, source_target_pairs={{0,2},{1,3},{2,0},{3,1},{4,6},{5,7},{6,4},{7,5},{8,10},{9,11},{10,... | collective-permute-start | bytes 2359304 | tf_op jit(solution)/shard_map/ppermute | solution.py:21
  36.0 19.8 %collective-permute-start.7 = (bf16[3,240,384]{2,1,0:T(8,128)(2,1)S(1)}, bf16[3,240,384]{2,1,0:T(8,128)(2,1)S(1)}, u32[]{:S(2)}, u32[]{:S(2)}) collective-permute-start(bf16[3,240,384]{2,1,0:T(8,128)(2,1)S(1)} %pad_maximum_fusion.5.refs_1_), channel_id=1, source_target_pairs={{0,4},{4,0},{1,5},{5,1},{2,6},{6,2},{3,7},{7,3},{8,12},{12,8},{9,1... | collective-permute-start | bytes 1658888 | tf_op jit(solution)/shard_map/ppermute | solution.py:21
  38.1 21.9 %collective-permute-start.13 = (bf16[192,384]{1,0:T(8,128)(2,1)S(1)}, bf16[192,384]{1,0:T(8,128)(2,1)S(1)}, u32[]{:S(2)}, u32[]{:S(2)}) collective-permute-start(bf16[192,384]{1,0:T(8,128)(2,1)S(1)} %bitcast.187), channel_id=1, source_target_pairs={{0,8},{8,0},{16,24},{24,16},{1,9},{9,1},{17,25},{25,17},{2,10},{10... | collective-permute-start | bytes 442376 | tf_op jit(solution)/shard_map/ppermute | solution.py:21
  39.9 21.4 %collective-permute-start.14 = (bf16[192,384]{1,0:T(8,128)(2,1)S(1)}, bf16[192,384]{1,0:T(8,128)(2,1)S(1)}, u32[]{:S(2)}, u32[]{:S(2)}) collective-permute-start(bf16[192,384]{1,0:T(8,128)(2,1)S(1)} %bitcast.188), channel_id=1, source_target_pairs={{0,16},{8,24},{16,0},{24,8},{1,17},{9,25},{17,1},{25,9},{2,18},{10... | collective-permute-start | bytes 442376 | tf_op jit(solution)/shard_map/ppermute | solution.py:21
  41.9 19.5 %collective-permute-start.15 = (bf16[192,384]{1,0:T(8,128)(2,1)S(1)}, bf16[192,384]{1,0:T(8,128)(2,1)}, u32[]{:S(2)}, u32[]{:S(2)}) collective-permute-start(bf16[192,384]{1,0:T(8,128)(2,1)S(1)} %bitcast.189), channel_id=1, source_target_pairs={{0,24},{8,16},{16,8},{24,0},{1,25},{9,17},{17,9},{25,1},{2,26},{10... | collective-permute-start | bytes 442376 | tf_op jit(solution)/shard_map/ppermute | solution.py:21
  55.8 17.8 %collective-permute-start.1 = (bf16[256,1536]{1,0:T(8,128)(2,1)S(1)}, bf16[256,1536]{1,0:T(8,128)(2,1)}, u32[]{:S(2)}, u32[]{:S(2)}) collective-permute-start(bf16[256,1536]{1,0:T(8,128)(2,1)S(1)} %bitcast.155), channel_id=1, source_target_pairs={{0,1},{1,0},{2,3},{3,2},{4,5},{5,4},{6,7},{7,6},{8,9},{9,8},{10,11... | collective-permute-start | bytes 2359304 | tf_op jit(solution)/shard_map/ppermute | solution.py:21
  60.0 8.9 %collective-permute-start.8 = (bf16[8,48,384]{2,1,0:T(8,128)(2,1)}, bf16[8,48,384]{2,1,0:T(8,128)(2,1)S(1)}, u32[]{:S(2)}, u32[]{:S(2)}) collective-permute-start(bf16[8,48,384]{2,1,0:T(8,128)(2,1)} %get-tuple-element.47), channel_id=1, source_target_pairs={{0,2},{1,3},{2,0},{3,1},{4,6},{5,7},{6,4},{7,5},{8,10},{9,11},{10,... | collective-permute-start | bytes 884744 | tf_op jit(solution)/shard_map/ppermute | solution.py:21
  62.4 6.7 %collective-permute-start.9 = (bf16[8,48,384]{2,1,0:T(8,128)(2,1)}, bf16[8,48,384]{2,1,0:T(8,128)(2,1)S(1)}, u32[]{:S(2)}, u32[]{:S(2)}) collective-permute-start(bf16[8,48,384]{2,1,0:T(8,128)(2,1)} %get-tuple-element.47), channel_id=1, source_target_pairs={{0,1},{1,0},{2,3},{3,2},{4,5},{5,4},{6,7},{7,6},{8,9},{9,8},{10,11... | collective-permute-start | bytes 884744 | tf_op jit(solution)/shard_map/ppermute | solution.py:21
  62.5 45.4 %collective-permute-start.16 = (bf16[4,192,384]{2,1,0:T(8,128)(2,1)S(1)}, bf16[4,192,384]{2,1,0:T(8,128)(2,1)S(1)}, u32[]{:S(2)}, u32[]{:S(2)}) collective-permute-start(bf16[4,192,384]{2,1,0:T(8,128)(2,1)S(1)} %pad_maximum_fusion.4.refs_0_), channel_id=1, source_target_pairs={{0,4},{4,0},{1,5},{5,1},{2,6},{6,2},{3,7},{7,3},{8,12},{12,8},{9,1... | collective-permute-start | bytes 1769480 | tf_op jit(solution)/shard_map/ppermute | solution.py:21
  65.2 8.4 %collective-permute-start.2 = (bf16[256,1536]{1,0:T(8,128)(2,1)S(1)}, bf16[256,1536]{1,0:T(8,128)(2,1)S(1)}, u32[]{:S(2)}, u32[]{:S(2)}) collective-permute-start(bf16[256,1536]{1,0:T(8,128)(2,1)S(1)} %collective-permute-done), channel_id=1, source_target_pairs={{0,1},{1,0},{2,3},{3,2},{4,5},{5,4},{6,7},{7,6},{8,9},{9,8},{10,11... | collective-permute-start | bytes 2359304 | tf_op jit(solution)/shard_map/ppermute | solution.py:21
  70.5 19.7 %collective-permute-start.11 = (bf16[256,1536]{1,0:T(8,128)(2,1)S(1)}, bf16[256,1536]{1,0:T(8,128)(2,1)}, u32[]{:S(2)}, u32[]{:S(2)}) collective-permute-start(bf16[256,1536]{1,0:T(8,128)(2,1)S(1)} %bitcast.148), channel_id=1, source_target_pairs={{0,2},{1,3},{2,0},{3,1},{4,6},{5,7},{6,4},{7,5},{8,10},{9,11},{10,... | collective-permute-start | bytes 2359304 | tf_op jit(solution)/shard_map/ppermute | solution.py:21
  82.4 15.7 %collective-permute-start.12 = (bf16[1024,256]{1,0:T(8,128)(2,1)S(1)}, bf16[1024,256]{1,0:T(8,128)(2,1)S(1)}, u32[]{:S(2)}, u32[]{:S(2)}) collective-permute-start(bf16[1024,256]{1,0:T(8,128)(2,1)S(1)} %convolution_convert_fusion.8.own_ref), channel_id=1, source_target_pairs={{0,4},{1,5},{2,6},{3,7},{8,12},{9,13},{10,14},{11,15},{16,20},{17,... | collective-permute-start | bytes 1572872 | tf_op jit(solution)/shard_map/ppermute | solution.py:27
  118.9 19.6 %collective-permute-start.18 = (bf16[256,1536]{1,0:T(8,128)(2,1)S(1)}, bf16[256,1536]{1,0:T(8,128)(2,1)S(1)}, u32[]{:S(2)}, u32[]{:S(2)}) collective-permute-start(bf16[256,1536]{1,0:T(8,128)(2,1)S(1)} %slice.292), channel_id=1, source_target_pairs={{0,2},{1,3},{2,0},{3,1},{4,6},{5,7},{6,4},{7,5},{8,10},{9,11},{10,... | collective-permute-start | bytes 2359304 | tf_op jit(solution)/shard_map/ppermute | solution.py:21
  139.1 19.0 %collective-permute-start.19 = (bf16[256,1536]{1,0:T(8,128)(2,1)S(1)}, bf16[256,1536]{1,0:T(8,128)(2,1)}, u32[]{:S(2)}, u32[]{:S(2)}) collective-permute-start(bf16[256,1536]{1,0:T(8,128)(2,1)S(1)} %multiply_convert_fusion.refs_0_), channel_id=1, source_target_pairs={{0,2},{1,3},{2,0},{3,1},{4,6},{5,7},{6,4},{7,5},{8,10},{9,11},{10,... | collective-permute-start | bytes 2359304 | tf_op jit(solution)/shard_map/ppermute | solution.py:21
  139.9 18.2 %collective-permute-start.22 = (bf16[256,1536]{1,0:T(8,128)(2,1)S(1)}, bf16[256,1536]{1,0:T(8,128)(2,1)}, u32[]{:S(2)}, u32[]{:S(2)}) collective-permute-start(bf16[256,1536]{1,0:T(8,128)(2,1)S(1)} %bitcast.149), channel_id=1, source_target_pairs={{0,1},{1,0},{2,3},{3,2},{4,5},{5,4},{6,7},{7,6},{8,9},{9,8},{10,11... | collective-permute-start | bytes 2359304 | tf_op jit(solution)/shard_map/ppermute | solution.py:21
  139.9 18.2 %collective-permute-start.23 = (bf16[256,1536]{1,0:T(8,128)(2,1)}, bf16[256,1536]{1,0:T(8,128)(2,1)}, u32[]{:S(2)}, u32[]{:S(2)}) collective-permute-start(bf16[256,1536]{1,0:T(8,128)(2,1)} %collective-permute-done.11.refs_5_), channel_id=1, source_target_pairs={{0,1},{1,0},{2,3},{3,2},{4,5},{5,4},{6,7},{7,6},{8,9},{9,8},{10,11... | collective-permute-start | bytes 2359304 | tf_op jit(solution)/shard_map/ppermute | solution.py:21
  140.4 17.7 %collective-permute-start.20 = (bf16[256,1536]{1,0:T(8,128)(2,1)S(1)}, bf16[256,1536]{1,0:T(8,128)(2,1)}, u32[]{:S(2)}, u32[]{:S(2)}) collective-permute-start(bf16[256,1536]{1,0:T(8,128)(2,1)S(1)} %multiply_convert_fusion.refs_0_), channel_id=1, source_target_pairs={{0,1},{1,0},{2,3},{3,2},{4,5},{5,4},{6,7},{7,6},{8,9},{9,8},{10,11... | collective-permute-start | bytes 2359304 | tf_op jit(solution)/shard_map/ppermute | solution.py:21
  217.9 40.3 %collective-permute-start.31 = (bf16[4,192,1152]{2,1,0:T(8,128)(2,1)}, bf16[4,192,1152]{2,1,0:T(8,128)(2,1)}, u32[]{:S(2)}, u32[]{:S(2)}) collective-permute-start(bf16[4,192,1152]{2,1,0:T(8,128)(2,1)} %dynamic-slice_bitcast_fusion.1), channel_id=1, source_target_pairs={{0,4},{4,0},{1,5},{5,1},{2,6},{6,2},{3,7},{7,3},{8,12},{12,8},{9,1... | collective-permute-start | bytes 5308424 | tf_op jit(solution)/shard_map/ppermute | solution.py:21
  237.0 12.5 %collective-permute-start.24 = (bf16[512,1536]{1,0:T(8,128)(2,1)S(1)}, bf16[512,1536]{1,0:T(8,128)(2,1)S(1)}, u32[]{:S(2)}, u32[]{:S(2)}) collective-permute-start(bf16[512,1536]{1,0:T(8,128)(2,1)S(1)} %fusion.16), channel_id=1, source_target_pairs={{0,1},{1,0},{2,3},{3,2},{4,5},{5,4},{6,7},{7,6},{8,9},{9,8},{10,11... | collective-permute-start | bytes 4718600 | tf_op jit(solution)/shard_map/ppermute | solution.py:21
  252.5 20.4 %collective-permute-start.25 = (bf16[256,1536]{1,0:T(8,128)(2,1)}, bf16[256,1536]{1,0:T(8,128)(2,1)S(1)}, u32[]{:S(2)}, u32[]{:S(2)}) collective-permute-start(bf16[256,1536]{1,0:T(8,128)(2,1)} %slice.291), channel_id=1, source_target_pairs={{0,2},{1,3},{2,0},{3,1},{4,6},{5,7},{6,4},{7,5},{8,10},{9,11},{10,... | collective-permute-start | bytes 2359304 | tf_op jit(solution)/shard_map/ppermute | solution.py:21
  261.3 175.6 %reduce-scatter.4.cloned.1.call-start = ((), (), s32[]{:S(2)}) async-start(), calls=%async_computation.4 | async-start | bytes 2211840 | tf_op jit(solution)/shard_map/reduce_scatter | solution.py:151
  272.4 39.3 %collective-permute-start.32 = (bf16[4,192,1152]{2,1,0:T(8,128)(2,1)}, bf16[4,192,1152]{2,1,0:T(8,128)(2,1)}, u32[]{:S(2)}, u32[]{:S(2)}) collective-permute-start(bf16[4,192,1152]{2,1,0:T(8,128)(2,1)} %get-tuple-element.65), channel_id=1, source_target_pairs={{0,4},{4,0},{1,5},{5,1},{2,6},{6,2},{3,7},{7,3},{8,12},{12,8},{9,1... | collective-permute-start | bytes 5308424 | tf_op jit(solution)/shard_map/ppermute | solution.py:21
  276.4 18.5 %collective-permute-start.26 = (bf16[256,1536]{1,0:T(8,128)(2,1)}, bf16[256,1536]{1,0:T(8,128)(2,1)}, u32[]{:S(2)}, u32[]{:S(2)}) collective-permute-start(bf16[256,1536]{1,0:T(8,128)(2,1)} %get-tuple-element.107), channel_id=1, source_target_pairs={{0,2},{1,3},{2,0},{3,1},{4,6},{5,7},{6,4},{7,5},{8,10},{9,11},{10,... | collective-permute-start | bytes 2359304 | tf_op jit(solution)/shard_map/ppermute | solution.py:21
  278.0 37.7 %collective-permute-start.29 = (bf16[256,1536]{1,0:T(8,128)(2,1)}, bf16[256,1536]{1,0:T(8,128)(2,1)}, u32[]{:S(2)}, u32[]{:S(2)}) collective-permute-start(bf16[256,1536]{1,0:T(8,128)(2,1)} %get-tuple-element.107), channel_id=1, source_target_pairs={{0,1},{1,0},{2,3},{3,2},{4,5},{5,4},{6,7},{7,6},{8,9},{9,8},{10,11... | collective-permute-start | bytes 2359304 | tf_op jit(solution)/shard_map/ppermute | solution.py:21
  294.9 20.8 %collective-permute-start.30 = (bf16[256,1536]{1,0:T(8,128)(2,1)}, bf16[256,1536]{1,0:T(8,128)(2,1)}, u32[]{:S(2)}, u32[]{:S(2)}) collective-permute-start(bf16[256,1536]{1,0:T(8,128)(2,1)} %collective-permute-done.26), channel_id=1, source_target_pairs={{0,1},{1,0},{2,3},{3,2},{4,5},{5,4},{6,7},{7,6},{8,9},{9,8},{10,11... | collective-permute-start | bytes 2359304 | tf_op jit(solution)/shard_map/ppermute | solution.py:21
  300.7 49.2 %collective-permute-start.27 = (bf16[512,1536]{1,0:T(8,128)(2,1)}, bf16[512,1536]{1,0:T(8,128)(2,1)}, u32[]{:S(2)}, u32[]{:S(2)}) collective-permute-start(bf16[512,1536]{1,0:T(8,128)(2,1)} %fusion.13), channel_id=1, source_target_pairs={{0,1},{1,0},{2,3},{3,2},{4,5},{5,4},{6,7},{7,6},{8,9},{9,8},{10,11... | collective-permute-start | bytes 4718600 | tf_op jit(solution)/shard_map/ppermute | solution.py:21
  311.7 47.1 %collective-permute-start.38 = (bf16[4,192,1152]{2,1,0:T(8,128)(2,1)}, bf16[4,192,1152]{2,1,0:T(8,128)(2,1)}, u32[]{:S(2)}, u32[]{:S(2)}) collective-permute-start(bf16[4,192,1152]{2,1,0:T(8,128)(2,1)} %get-tuple-element.73), channel_id=1, source_target_pairs={{0,4},{4,0},{1,5},{5,1},{2,6},{6,2},{3,7},{7,3},{8,12},{12,8},{9,1... | collective-permute-start | bytes 5308424 | tf_op jit(solution)/shard_map/ppermute | solution.py:21
  315.4 123.5 %reduce-scatter.6.cloned.1.call-start = ((), (), s32[]{:S(2)}) async-start(), calls=%async_computation.5 | async-start | bytes 2211840 | tf_op jit(solution)/shard_map/reduce_scatter | solution.py:151
  339.3 8.7 %collective-permute-start.36 = (bf16[256,512]{1,0:T(8,128)(2,1)S(1)}, bf16[256,512]{1,0:T(8,128)(2,1)S(1)}, u32[]{:S(2)}, u32[]{:S(2)}) collective-permute-start(bf16[256,512]{1,0:T(8,128)(2,1)S(1)} %slice.295), channel_id=1, source_target_pairs={{0,2},{1,3},{2,0},{3,1},{4,6},{5,7},{6,4},{7,5},{8,10},{9,11},{10,... | collective-permute-start | bytes 786440 | tf_op jit(solution)/shard_map/ppermute | solution.py:21
  343.0 26.0 %collective-permute-start.33 = (bf16[512,1536]{1,0:T(8,128)(2,1)}, bf16[512,1536]{1,0:T(8,128)(2,1)}, u32[]{:S(2)}, u32[]{:S(2)}) collective-permute-start(bf16[512,1536]{1,0:T(8,128)(2,1)} %convolution_convert_fusion.3), channel_id=1, source_target_pairs={{0,1},{1,0},{2,3},{3,2},{4,5},{5,4},{6,7},{7,6},{8,9},{9,8},{10,11... | collective-permute-start | bytes 4718600 | tf_op jit(solution)/shard_map/ppermute | solution.py:21
  348.2 8.9 %collective-permute-start.37 = (bf16[256,256]{1,0:T(8,128)(2,1)S(1)}, bf16[256,256]{1,0:T(8,128)(2,1)S(1)}, u32[]{:S(2)}, u32[]{:S(2)}) collective-permute-start(bf16[256,256]{1,0:T(8,128)(2,1)S(1)} %slice.296), channel_id=1, source_target_pairs={{4,0},{5,1},{6,2},{7,3},{12,8},{13,9},{14,10},{15,11},{20,16},{21,... | collective-permute-start | bytes 393224 | tf_op jit(solution)/shard_map/ppermute | solution.py:27
  355.6 20.3 %collective-permute-start.28 = (bf16[256,1536]{1,0:T(8,128)(2,1)}, bf16[256,1536]{1,0:T(8,128)(2,1)S(1)}, u32[]{:S(2)}, u32[]{:S(2)}) collective-permute-start(bf16[256,1536]{1,0:T(8,128)(2,1)} %slice.290), channel_id=1, source_target_pairs={{0,2},{1,3},{2,0},{3,1},{4,6},{5,7},{6,4},{7,5},{8,10},{9,11},{10,... | collective-permute-start | bytes 2359304 | tf_op jit(solution)/shard_map/ppermute | solution.py:21
  361.1 11.9 %collective-permute-start.40 = (bf16[2,8,48,384]{3,2,1,0:T(8,128)(2,1)}, bf16[2,8,48,384]{3,2,1,0:T(8,128)(2,1)}, u32[]{:S(2)}, u32[]{:S(2)}) collective-permute-start(bf16[2,8,48,384]{3,2,1,0:T(8,128)(2,1)} %slice.293), channel_id=1, source_target_pairs={{0,1},{1,0},{2,3},{3,2},{4,5},{5,4},{6,7},{7,6},{8,9},{9,8},{10,11... | collective-permute-start | bytes 1769480 | tf_op jit(solution)/shard_map/ppermute | solution.py:21
  361.1 47.4 %collective-permute-start.39 = (bf16[4,384,384]{2,1,0:T(8,128)(2,1)}, bf16[4,384,384]{2,1,0:T(8,128)(2,1)}, u32[]{:S(2)}, u32[]{:S(2)}) collective-permute-start(bf16[4,384,384]{2,1,0:T(8,128)(2,1)} %fusion.34), channel_id=1, source_target_pairs={{0,4},{4,0},{1,5},{5,1},{2,6},{6,2},{3,7},{7,3},{8,12},{12,8},{9,1... | collective-permute-start | bytes 3538952 | tf_op jit(solution)/shard_map/ppermute | solution.py:21
  372.0 28.7 %collective-permute-start.34 = (bf16[256,1536]{1,0:T(8,128)(2,1)S(1)}, bf16[256,1536]{1,0:T(8,128)(2,1)S(1)}, u32[]{:S(2)}, u32[]{:S(2)}) collective-permute-start(bf16[256,1536]{1,0:T(8,128)(2,1)S(1)} %slice.289), channel_id=1, source_target_pairs={{0,2},{1,3},{2,0},{3,1},{4,6},{5,7},{6,4},{7,5},{8,10},{9,11},{10,... | collective-permute-start | bytes 2359304 | tf_op jit(solution)/shard_map/ppermute | solution.py:21
  374.7 23.5 %collective-permute-start.41 = (bf16[1,8,48,384]{3,2,1,0:T(8,128)(2,1)S(1)}, bf16[1,8,48,384]{3,2,1,0:T(8,128)(2,1)S(1)}, u32[]{:S(2)}, u32[]{:S(2)}) collective-permute-start(bf16[1,8,48,384]{3,2,1,0:T(8,128)(2,1)S(1)} %slice.294), channel_id=1, source_target_pairs={{0,2},{1,3},{2,0},{3,1},{4,6},{5,7},{6,4},{7,5},{8,10},{9,11},{10,... | collective-permute-start | bytes 884744 | tf_op jit(solution)/shard_map/ppermute | solution.py:21
  404.0 6.9 %collective-permute-start.43 = (bf16[48,384]{1,0:T(8,128)(2,1)S(1)}, bf16[48,384]{1,0:T(8,128)(2,1)S(1)}, u32[]{:S(2)}, u32[]{:S(2)}) collective-permute-start(bf16[48,384]{1,0:T(8,128)(2,1)S(1)} %get-tuple-element.77), channel_id=1, source_target_pairs={{0,8},{8,0},{16,24},{24,16},{1,9},{9,1},{17,25},{25,17},{2,10},{10... | collective-permute-start | bytes 110600 | tf_op jit(solution)/shard_map/ppermute | solution.py:21
  404.3 6.6 %collective-permute-start.44 = (bf16[48,384]{1,0:T(8,128)(2,1)S(1)}, bf16[48,384]{1,0:T(8,128)(2,1)S(1)}, u32[]{:S(2)}, u32[]{:S(2)}) collective-permute-start(bf16[48,384]{1,0:T(8,128)(2,1)S(1)} %get-tuple-element.78), channel_id=1, source_target_pairs={{0,16},{8,24},{16,0},{24,8},{1,17},{9,25},{17,1},{25,9},{2,18},{10... | collective-permute-start | bytes 110600 | tf_op jit(solution)/shard_map/ppermute | solution.py:21
  407.3 6.2 %collective-permute-start.45 = (bf16[48,384]{1,0:T(8,128)(2,1)S(1)}, bf16[48,384]{1,0:T(8,128)(2,1)S(1)}, u32[]{:S(2)}, u32[]{:S(2)}) collective-permute-start(bf16[48,384]{1,0:T(8,128)(2,1)S(1)} %get-tuple-element.79), channel_id=1, source_target_pairs={{0,24},{8,16},{16,8},{24,0},{1,25},{9,17},{17,9},{25,1},{2,26},{10... | collective-permute-start | bytes 110600 | tf_op jit(solution)/shard_map/ppermute | solution.py:21
  413.5 11.5 %collective-permute-start.46 = (bf16[384,384]{1,0:T(8,128)(2,1)}, bf16[384,384]{1,0:T(8,128)(2,1)S(1)}, u32[]{:S(2)}, u32[]{:S(2)}) collective-permute-start(bf16[384,384]{1,0:T(8,128)(2,1)} %get-tuple-element.80), channel_id=1, source_target_pairs={{0,8},{8,0},{16,24},{24,16},{1,9},{9,1},{17,25},{25,17},{2,10},{10... | collective-permute-start | bytes 884744 | tf_op jit(solution)/shard_map/ppermute | solution.py:21
  413.5 22.4 %collective-permute-start.47 = (bf16[384,384]{1,0:T(8,128)(2,1)}, bf16[384,384]{1,0:T(8,128)(2,1)S(1)}, u32[]{:S(2)}, u32[]{:S(2)}) collective-permute-start(bf16[384,384]{1,0:T(8,128)(2,1)} %get-tuple-element.81), channel_id=1, source_target_pairs={{0,16},{8,24},{16,0},{24,8},{1,17},{9,25},{17,1},{25,9},{2,18},{10... | collective-permute-start | bytes 884744 | tf_op jit(solution)/shard_map/ppermute | solution.py:21
  414.7 21.2 %collective-permute-start.48 = (bf16[384,384]{1,0:T(8,128)(2,1)S(1)}, bf16[384,384]{1,0:T(8,128)(2,1)S(1)}, u32[]{:S(2)}, u32[]{:S(2)}) collective-permute-start(bf16[384,384]{1,0:T(8,128)(2,1)S(1)} %get-tuple-element.82), channel_id=1, source_target_pairs={{0,24},{8,16},{16,8},{24,0},{1,25},{9,17},{17,9},{25,1},{2,26},{10... | collective-permute-start | bytes 884744 | tf_op jit(solution)/shard_map/ppermute | solution.py:21
  (66 other events, 622.2 us)
Sparse Core Ops, SparseCore 0:
  29.3 163.0 all-gather.1
  261.4 37.0 reduce-scatter.7
  315.5 38.6 reduce-scatter.3
  367.1 37.1 reduce-scatter.5
where the time goes:
time: 456 us; the launch traced here: 448 us
  waiting for transfers between devices  190 us (42%)
  matrix products  63.7 us (14%)
  Pallas kernels  56 us (12%)
  starting transfers between devices  53.7 us (12%)
  other arithmetic  44.3 us (10%)
  local copies, waits for them, and re-layouts  24.4 us (5%)
  between operations  15.2 us (3%)
    ppermute x47, waiting for transfers between devices, swap(): return lax.ppermute(value, axis, [(i, i ^ k) for i in range(count)])  151 us
    ppermute x47, starting transfers between devices, swap(): return lax.ppermute(value, axis, [(i, i ^ k) for i in range(count)])  46.8 us
    dot_general x9, matrix products, dot_nt(): lax.dot_general(a, b, (((1,), (1,)), ((), ())), preferred_element_type=F32)  32.2 us
    all_gather x1, waiting for transfers between devices, local(): lax.all_gather(after(gate_up, *first_along), both, axis=0, tiled=True)  31.6 us
    dot_general x6, matrix products, mm_tn(): lax.dot_general(a, b, (((0,), (0,)), ((), ())), preferred_element_type=F32)  27 us
    pallas_call x1, Pallas kernels, ffn_forward(): pl.pallas_call(functools.partial(ffn_forward_kernel, count), grid=(count,...  17 us
    pallas_call x1, Pallas kernels, attention_backward(): pl.pallas_call(attend_backward, grid_spec=pltpu.PrefetchScalarGridSpec(nu...  15.2 us
    unnamed x124, local copies, waits for them, and re-layouts  11.6 us
  transfers between devices with their start and end apart: 53, of which 22 were waited for; matrix products, arithmetic and copies ran while one was open for 25% of the time, Pallas kernels for 9%

commit v1 on v0

--- a/solution.py
+++ b/solution.py
@@ -558,8 +558,9 @@
     part_gate = slabs_of(mm_tn(after(second_rows, two_away, two_own), grads[:, :ff]).astype(BF))
     got_down = behind(got_down, part_gate)
     grad_down = rest_large(half_sum(part_down, got_down))
-    got_gate = half_sent(part_gate, got_down)
-    part_up = slabs_of(mm_tn(after(second_rows, part_gate), grads[:, ff:]).astype(BF))
+    sent_gate = behind(away_half(part_gate), *got_down)
+    got_gate = [swap(x, "context", k + 1) for k, x in enumerate(sent_gate)]
+    part_up = slabs_of(mm_tn(after(second_rows, *sent_gate), grads[:, ff:]).astype(BF))
 
     gain_two_part = jnp.sum(d_two * middle * inv_two, axis=0, keepdims=True)
     d_middle = cotangent.astype(F32) + norm_backward(d_two, middle, inv_two, gain_two)

time: 456 us -> 451 us (0.989)
  waiting for transfers between devices: 190 us -> 181 us
  other arithmetic: 44.3 us -> 50.4 us
    ppermute x47, waiting for transfers between devices: 151 us -> 141 us  [swap(): return lax.ppermute(value, axis, [(i, i ^ k) for i in range(count)])]
    unnamed x124 -> x126, local copies, waits for them, and re-layouts: 11.6 us -> 10.5 us
  transfers between devices with their start and end apart: 53 -> 53, of which waited for: 22 -> 23; matrix products, arithmetic and copies ran while one was open for 25% -> 26% of each run, Pallas kernels for 9% -> 9%
where the time goes in v1:
time: 451 us; the launch traced here: 443 us
  waiting for transfers between devices  181 us (40%)
  matrix products  61.3 us (14%)
  Pallas kernels  57.1 us (13%)
  starting transfers between devices  52.8 us (12%)
  other arithmetic  50.4 us (11%)
  local copies, waits for them, and re-layouts  25.5 us (6%)
  between operations  15.2 us (3%)
    ppermute x47, waiting for transfers between devices, swap(): return lax.ppermute(value, axis, [(i, i ^ k) for i in range(count)])  141 us
    ppermute x47, starting transfers between devices, swap(): return lax.ppermute(value, axis, [(i, i ^ k) for i in range(count)])  46.2 us
    all_gather x1, waiting for transfers between devices, local(): lax.all_gather(after(gate_up, *first_along), both, axis=0, tiled=True)  33 us
    dot_general x9, matrix products, dot_nt(): lax.dot_general(a, b, (((1,), (1,)), ((), ())), preferred_element_type=F32)  31.9 us
    dot_general x6, matrix products, mm_tn(): lax.dot_general(a, b, (((0,), (0,)), ((), ())), preferred_element_type=F32)  24.9 us
    pallas_call x1, Pallas kernels, ffn_forward(): pl.pallas_call(functools.partial(ffn_forward_kernel, count), grid=(count,...  17.8 us
    pallas_call x1, Pallas kernels, attention_backward(): pl.pallas_call(attend_backward, grid_spec=pltpu.PrefetchScalarGridSpec(nu...  15.6 us
    unnamed x126, local copies, waits for them, and re-layouts  10.5 us
  transfers between devices with their start and end apart: 53, of which 23 were waited for; matrix products, arithmetic and copies ran while one was open for 26% of the time, Pallas kernels for 9%

profile of v1, /device:TPU:0, one launch (start us, length us, event | category | flops | bytes accessed | tf_op | source)
XLA Modules:
  0.0 443.1 jit_solution(2967696947453647125)
XLA Ops:
  9.7 3.0 collective-permute-start.3
  12.8 2.6 collective-permute-start.4
  15.4 2.6 pad_maximum_fusion.3
  18.0 2.5 collective-permute-done.3
  20.5 8.7 %collective-permute-done.4 = bf16[240,384]{1,0:T(8,128)(2,1)S(1)} collective-permute-done((bf16[240,384]{1,0:T(8,128)(2,1)S(1)}, bf16[240,384]{1,0:T(8,128)(2,1)S(1)}, u32[]{:S(2)}, u32[]{:S(2)}) %collective-permute-start.4) | collective-permute-done | bytes 184352 | tf_op jit(solution)/shard_map/ppermute | solution.py:21
  32.4 3.6 collective-permute-done.6
  42.5 13.4 %collective-permute-done.7.refs_3_ = bf16[3,240,384]{2,1,0:T(8,128)(2,1)} collective-permute-done((bf16[3,240,384]{2,1,0:T(8,128)(2,1)S(1)}, bf16[3,240,384]{2,1,0:T(8,128)(2,1)}, u32[]{:S(2)}, u32[]{:S(2)}) %collective-permute-start.7) | collective-permute-done | bytes 552992 | tf_op jit(solution)/shard_map/ppermute | solution.py:21
  55.8 3.3 place.2
  61.9 2.6 collective-permute-start.16
  64.8 4.1 collective-permute-done.8
  74.4 5.6 %fusion.2 = bf16[1024,1536]{1,0:T(8,128)(2,1)S(1)} fusion(f32[1536]{0:T(1024)S(1)} %get-tuple-element.106, f32[1024]{0:T(1024)S(1)} %add_rsqrt_fusion, bf16[256,1536]{1,0:T(8,128)(2,1)S(1)} %collective-permute-done.2, bf16[256,1536]{1,0:T(8,128)(2,1)S(1)} %collective-permute-done.1, bf16[256,1536]{1,0:T(8,128)(2,1)S(1)} %collective-permute-done, ...), kind=kLoop, calls=%fused_computation.7 | loop fusion | flops 17301504 | bytes 6301696 | tf_op jit(solution)/shard_map/convert_element_type | solution.py:534
  81.1 4.8 %collective-permute-start.12 = (bf16[1024,256]{1,0:T(8,128)(2,1)S(1)}, bf16[1024,256]{1,0:T(8,128)(2,1)S(1)}, u32[]{:S(2)}, u32[]{:S(2)}) collective-permute-start(bf16[1024,256]{1,0:T(8,128)(2,1)S(1)} %convolution_convert_fusion.8.own_ref), channel_id=1, source_target_pairs={{0,4},{1,5},{2,6},{3,7},{8,12},{9,13},{10,14},{11,15},{16,20},{17,... | collective-permute-start | bytes 1572872 | tf_op jit(solution)/shard_map/ppermute | solution.py:27
  87.7 2.4 collective-permute-done.11.refs_5_
  90.2 6.7 %collective-permute-done.12.prev_ref = bf16[1024,256]{1,0:T(8,128)(2,1)S(1)} collective-permute-done((bf16[1024,256]{1,0:T(8,128)(2,1)S(1)}, bf16[1024,256]{1,0:T(8,128)(2,1)S(1)}, u32[]{:S(2)}, u32[]{:S(2)}) %collective-permute-start.12) | collective-permute-done | bytes 524320 | tf_op jit(solution)/shard_map/ppermute | solution.py:27
  97.2 9.2 %attend_forward.1 = (bf16[1024,384]{1,0:T(8,128)(2,1)S(1)}, f32[3,1024]{1,0:T(4,128)S(1)}) custom-call(s32[4]{0:T(128)S(1)} %broadcast_xor_fusion.blocks_ref, bf16[1024,384]{1,0:T(8,128)(2,1)S(1)} %convolution_convert_fusion.7.q_ref, bf16[1024,256]{1,0:T(8,128)(2,1)S(1)} %collective-permute-done.12.prev_ref, ...), custom_call_target="tpu_custom_call" | custom-call | flops 1 | bytes 1 | tf_op jit(solution)/shard_map/attend_forward/pallas_call | solution.py:289
  107.4 3.2 place.3
  113.0 3.4 collective-permute-done.17
  118.3 18.8 %collective-permute-done.18 = bf16[256,1536]{1,0:T(8,128)(2,1)S(1)} collective-permute-done((bf16[256,1536]{1,0:T(8,128)(2,1)S(1)}, bf16[256,1536]{1,0:T(8,128)(2,1)S(1)}, u32[]{:S(2)}, u32[]{:S(2)}) %collective-permute-start.18) | collective-permute-done | bytes 786464 | tf_op jit(solution)/shard_map/ppermute | solution.py:21
  139.1 17.7 %collective-permute-done.19.refs_1_ = bf16[256,1536]{1,0:T(8,128)(2,1)} collective-permute-done((bf16[256,1536]{1,0:T(8,128)(2,1)S(1)}, bf16[256,1536]{1,0:T(8,128)(2,1)}, u32[]{:S(2)}, u32[]{:S(2)}) %collective-permute-start.19) | collective-permute-done | bytes 786464 | tf_op jit(solution)/shard_map/ppermute | solution.py:21
  156.9 2.5 collective-permute-done.21.refs_3_
  159.4 33.0 %all-gather.2.cloned.1.call-done.refs_8_.refs_9_.down = bf16[1536,3456]{1,0:T(8,128)(2,1)} async-done(((bf16[192,3456]{1,0:T(8,128)(2,1)}), bf16[1536,3456]{1,0:T(8,128)(2,1)}) %all-gather.2.cloned.1.call-update) | async-done | bytes 10616848 | tf_op jit(solution)/shard_map/all_gather | solution.py:504
  192.5 17.8 %ffn_forward.1 = (bf16[1024,1152]{1,0:T(8,128)(2,1)}, bf16[1024,1152]{1,0:T(8,128)(2,1)}, bf16[1024,1152]{1,0:T(8,128)(2,1)}, bf16[1024,1536]{1,0:T(8,128)(2,1)}, bf16[1024,1536]{1,0:T(8,128)(2,1)}) custom-call(bf16[256,1536]{1,0:T(8,128)(2,1)S(1)} %multiply_convert_fusion.refs_0_, bf16[256,1536]{1,0:T(8,128)(2,1)} %collective-permute-done.19.refs_1_, ...), custom_call_target="tpu_custom_call" | custom-call | flops 7247757312 | bytes 20971520 | tf_op jit(solution)/shard_map/ffn_forward/pallas_call | solution.py:411
  210.3 7.1 %convolution_convert_fusion.2 = bf16[1536,1152]{1,0:T(8,128)(2,1)S(1)} fusion(bf16[1024,1536]{1,0:T(8,128)(2,1)} %get-tuple-element.58.cot, bf16[1024,1152]{1,0:T(8,128)(2,1)} %get-tuple-element.61), kind=kOutput, calls=%fused_computation.4 | convolution fusion | flops 3625648128 | bytes 9043968 | tf_op jit(solution)/shard_map/dot_general | solution.py:471
  221.2 8.0 %ffn_backward.1 = bf16[1024,2304]{1,0:T(8,128)(2,1)S(1)} custom-call(bf16[1024,1536]{1,0:T(8,128)(2,1)S(1)} %copy-done.1, bf16[1024,1152]{1,0:T(8,128)(2,1)S(1)} %copy-done.3, bf16[1024,1152]{1,0:T(8,128)(2,1)S(1)} %copy-done.4, bf16[1536,3456]{1,0:T(8,128)(2,1)} %all-gather.2.cloned.1.call-done.refs_8_.refs_9_.down), custom_call_target="tpu_custom_call" | custom-call | flops 3623878656 | bytes 16777216 | tf_op jit(solution)/shard_map/ffn_backward/pallas_call | solution.py:444
  229.2 8.6 %fusion.16 = bf16[512,1536]{1,0:T(8,128)(2,1)S(1)} fusion(bf16[1536,3456]{1,0:T(8,128)(2,1)} %all-gather.2.cloned.1.call-done.refs_8_.refs_9_.down, bf16[1024,2304]{1,0:T(8,128)(2,1)S(1)} %ffn_backward.1), kind=kOutput, calls=%fused_computation.28 | convolution fusion | flops 3624665088 | bytes 11010048 | tf_op jit(solution)/shard_map/dot_general | solution.py:167
  238.0 3.8 fusion.5
  241.8 8.9 %convolution_convert_fusion.1 = bf16[1536,1152]{1,0:T(8,128)(2,1)} fusion(bf16[1024,1536]{1,0:T(8,128)(2,1)} %get-tuple-element.66, bf16[1024,2304]{1,0:T(8,128)(2,1)S(1)} %ffn_backward.1), kind=kOutput, calls=%fused_computation.3 | convolution fusion | flops 3625648128 | bytes 9043968 | tf_op jit(solution)/shard_map/dot_general | solution.py:471
  255.2 3.9 collective-permute-done.31
  259.1 3.2 fusion.7
  262.3 3.0 dynamic-slice_bitcast_fusion.2
  265.8 8.2 %collective-permute-done.25 = bf16[256,1536]{1,0:T(8,128)(2,1)S(1)} collective-permute-done((bf16[256,1536]{1,0:T(8,128)(2,1)}, bf16[256,1536]{1,0:T(8,128)(2,1)S(1)}, u32[]{:S(2)}, u32[]{:S(2)}) %collective-permute-start.25) | collective-permute-done | bytes 786464 | tf_op jit(solution)/shard_map/ppermute | solution.py:21
  273.9 2.7 multiply_reduce_fusion.1
  276.7 3.6 fusion.63
  281.6 4.5 %convolution_convert_fusion = bf16[1536,1152]{1,0:T(8,128)(2,1)S(1)} fusion(bf16[1024,1536]{1,0:T(8,128)(2,1)S(1)} %copy-done.54, bf16[1024,2304]{1,0:T(8,128)(2,1)S(1)} %bitcast.149), kind=kOutput, calls=%fused_computation.2 | convolution fusion | flops 3625648128 | bytes 9043968 | tf_op jit(solution)/shard_map/dot_general | solution.py:471
  290.8 8.7 %collective-permute-done.26 = bf16[256,1536]{1,0:T(8,128)(2,1)S(1)} collective-permute-done((bf16[256,1536]{1,0:T(8,128)(2,1)S(1)}, bf16[256,1536]{1,0:T(8,128)(2,1)S(1)}, u32[]{:S(2)}, u32[]{:S(2)}) %collective-permute-start.26) | collective-permute-done | bytes 786464 | tf_op jit(solution)/shard_map/ppermute | solution.py:21
  299.5 5.7 %fusion.13 = bf16[512,1536]{1,0:T(8,128)(2,1)} fusion(bf16[1536,3456]{1,0:T(8,128)(2,1)} %all-gather.2.cloned.1.call-done.refs_8_.refs_9_.down, bf16[1024,1152]{1,0:T(8,128)(2,1)} %get-tuple-element.61), kind=kOutput, calls=%fused_computation.27 | convolution fusion | flops 1812725760 | bytes 6291456 | tf_op jit(solution)/shard_map/dot_general | solution.py:167
  306.2 3.3 fusion.9
  309.6 4.6 %pad_maximum_fusion.1 = bf16[1024,1536]{1,0:T(8,128)(2,1)S(1)} fusion(bf16[256,1536]{1,0:T(8,128)(2,1)} %collective-permute-done.30, bf16[256,1536]{1,0:T(8,128)(2,1)} %collective-permute-done.29, bf16[256,1536]{1,0:T(8,128)(2,1)S(1)} %collective-permute-done.26, bf16[256,1536]{1,0:T(8,128)(2,1)S(1)} %get-tuple-element.107), kind=kLoop, calls=%fused_computation.22 | loop fusion | flops 12582912 | bytes 6291456 | tf_op jit(solution)/shard_map/concatenate | solution.py:571
  316.0 15.6 %attend_backward.1 = (bf16[1024,384]{1,0:T(8,128)(2,1)S(1)}, bf16[1024,512]{1,0:T(8,128)(2,1)S(1)}) custom-call(s32[4]{0:T(128)S(1)} %broadcast_xor_fusion.blocks_ref, bf16[1024,384]{1,0:T(8,128)(2,1)S(1)} %convolution_convert_fusion.7.q_ref, bf16[1024,256]{1,0:T(8,128)(2,1)S(1)} %copy-done.8, bf16[1024,256]{1,0:T(8,128)(2,1)S(1)} %copy-done.6, ...), custom_call_target="tpu_custom_call" | custom-call | flops 1 | bytes 1 | tf_op jit(solution)/shard_map/attend_backward/pallas_call | solution.py:322
  341.3 3.7 collective-permute-done.36
  346.8 4.7 %convolution_add_fusion.2 = f32[512,1536]{1,0:T(8,128)S(1)} fusion(bf16[512,1536]{1,0:T(8,128)(2,1)} %collective-permute-done.27, bf16[1536,3456]{1,0:T(8,128)(2,1)} %all-gather.2.cloned.1.call-done.refs_8_.refs_9_.down, bf16[1024,1152]{1,0:T(8,128)(2,1)S(1)} %copy-done.55), kind=kOutput, calls=%fused_computation.20 | convolution fusion | flops 1813512192 | bytes 9437184 | tf_op jit(solution)/shard_map/dot_general | solution.py:167
  357.9 2.6 collective-permute-start.39
  360.6 3.2 fusion.8
  365.8 2.6 convolution_add_fusion
  374.9 20.2 %collective-permute-done.41 = bf16[1,8,48,384]{3,2,1,0:T(8,128)(2,1)S(1)} collective-permute-done((bf16[1,8,48,384]{3,2,1,0:T(8,128)(2,1)S(1)}, bf16[1,8,48,384]{3,2,1,0:T(8,128)(2,1)S(1)}, u32[]{:S(2)}, u32[]{:S(2)}) %collective-permute-start.41) | collective-permute-done | bytes 294944 | tf_op jit(solution)/shard_map/ppermute | solution.py:21
  409.0 2.8 collective-permute-start.47
  416.0 6.2 %collective-permute-done.46 = bf16[384,384]{1,0:T(8,128)(2,1)S(1)} collective-permute-done((bf16[384,384]{1,0:T(8,128)(2,1)}, bf16[384,384]{1,0:T(8,128)(2,1)S(1)}, u32[]{:S(2)}, u32[]{:S(2)}) %collective-permute-start.46) | collective-permute-done | bytes 294944 | tf_op jit(solution)/shard_map/ppermute | solution.py:21
  422.2 9.1 %collective-permute-done.47 = bf16[384,384]{1,0:T(8,128)(2,1)S(1)} collective-permute-done((bf16[384,384]{1,0:T(8,128)(2,1)}, bf16[384,384]{1,0:T(8,128)(2,1)S(1)}, u32[]{:S(2)}, u32[]{:S(2)}) %collective-permute-start.47) | collective-permute-done | bytes 294944 | tf_op jit(solution)/shard_map/ppermute | solution.py:21
  (288 shorter events, 97.8 us)
Async XLA Ops:
  7.2 185.3 %all-gather.2.cloned.1.call-start = ((), (), s32[]{:S(2)}) async-start(), calls=%async_computation.3 | async-start | bytes 11943936 | tf_op jit(solution)/shard_map/all_gather | solution.py:504
  9.7 10.7 %collective-permute-start.3 = (bf16[240,384]{1,0:T(8,128)(2,1)S(1)}, bf16[240,384]{1,0:T(8,128)(2,1)S(1)}, u32[]{:S(2)}, u32[]{:S(2)}) collective-permute-start(bf16[240,384]{1,0:T(8,128)(2,1)S(1)} %get-tuple-element.128), channel_id=1, source_target_pairs={{0,8},{8,0},{16,24},{24,16},{1,9},{9,1},{17,25},{25,17},{2,10},{10... | collective-permute-start | bytes 552968 | tf_op jit(solution)/shard_map/ppermute | solution.py:21
  12.8 16.4 %collective-permute-start.4 = (bf16[240,384]{1,0:T(8,128)(2,1)S(1)}, bf16[240,384]{1,0:T(8,128)(2,1)S(1)}, u32[]{:S(2)}, u32[]{:S(2)}) collective-permute-start(bf16[240,384]{1,0:T(8,128)(2,1)S(1)} %get-tuple-element.128), channel_id=1, source_target_pairs={{0,16},{8,24},{16,0},{24,8},{1,17},{9,25},{17,1},{25,9},{2,18},{10... | collective-permute-start | bytes 552968 | tf_op jit(solution)/shard_map/ppermute | solution.py:21
  15.4 13.8 %collective-permute-start.5 = (bf16[240,384]{1,0:T(8,128)(2,1)S(1)}, bf16[240,384]{1,0:T(8,128)(2,1)S(1)}, u32[]{:S(2)}, u32[]{:S(2)}) collective-permute-start(bf16[240,384]{1,0:T(8,128)(2,1)S(1)} %get-tuple-element.128), channel_id=1, source_target_pairs={{0,24},{8,16},{16,8},{24,0},{1,25},{9,17},{17,9},{25,1},{2,26},{10... | collective-permute-start | bytes 552968 | tf_op jit(solution)/shard_map/ppermute | solution.py:21
  29.2 334.7 %reduce-scatter.8.cloned.1.call-start = ((), (), s32[]{:S(2)}) async-start(), calls=%async_computation.6 | async-start | bytes 2211840 | tf_op jit(solution)/shard_map/reduce_scatter | solution.py:151
  29.2 6.8 %collective-permute-start.6 = (bf16[240,384]{1,0:T(8,128)(2,1)S(1)}, bf16[240,384]{1,0:T(8,128)(2,1)S(1)}, u32[]{:S(2)}, u32[]{:S(2)}) collective-permute-start(bf16[240,384]{1,0:T(8,128)(2,1)S(1)} %get-tuple-element.128), channel_id=1, source_target_pairs={{0,4},{4,0},{1,5},{5,1},{2,6},{6,2},{3,7},{7,3},{8,12},{12,8},{9,1... | collective-permute-start | bytes 552968 | tf_op jit(solution)/shard_map/ppermute | solution.py:21
  30.8 33.9 %collective-permute-start = (bf16[256,1536]{1,0:T(8,128)(2,1)S(1)}, bf16[256,1536]{1,0:T(8,128)(2,1)S(1)}, u32[]{:S(2)}, u32[]{:S(2)}) collective-permute-start(bf16[256,1536]{1,0:T(8,128)(2,1)S(1)} %bitcast.156), channel_id=1, source_target_pairs={{0,2},{1,3},{2,0},{3,1},{4,6},{5,7},{6,4},{7,5},{8,10},{9,11},{10,... | collective-permute-start | bytes 2359304 | tf_op jit(solution)/shard_map/ppermute | solution.py:21
  36.0 19.8 %collective-permute-start.7 = (bf16[3,240,384]{2,1,0:T(8,128)(2,1)S(1)}, bf16[3,240,384]{2,1,0:T(8,128)(2,1)}, u32[]{:S(2)}, u32[]{:S(2)}) collective-permute-start(bf16[3,240,384]{2,1,0:T(8,128)(2,1)S(1)} %pad_maximum_fusion.5.refs_1_), channel_id=1, source_target_pairs={{0,4},{4,0},{1,5},{5,1},{2,6},{6,2},{3,7},{7,3},{8,12},{12,8},{9,1... | collective-permute-start | bytes 1658888 | tf_op jit(solution)/shard_map/ppermute | solution.py:21
  38.1 21.1 %collective-permute-start.13 = (bf16[192,384]{1,0:T(8,128)(2,1)S(1)}, bf16[192,384]{1,0:T(8,128)(2,1)S(1)}, u32[]{:S(2)}, u32[]{:S(2)}) collective-permute-start(bf16[192,384]{1,0:T(8,128)(2,1)S(1)} %bitcast.189), channel_id=1, source_target_pairs={{0,8},{8,0},{16,24},{24,16},{1,9},{9,1},{17,25},{25,17},{2,10},{10... | collective-permute-start | bytes 442376 | tf_op jit(solution)/shard_map/ppermute | solution.py:21
  39.9 20.6 %collective-permute-start.14 = (bf16[192,384]{1,0:T(8,128)(2,1)S(1)}, bf16[192,384]{1,0:T(8,128)(2,1)}, u32[]{:S(2)}, u32[]{:S(2)}) collective-permute-start(bf16[192,384]{1,0:T(8,128)(2,1)S(1)} %bitcast.190), channel_id=1, source_target_pairs={{0,16},{8,24},{16,0},{24,8},{1,17},{9,25},{17,1},{25,9},{2,18},{10... | collective-permute-start | bytes 442376 | tf_op jit(solution)/shard_map/ppermute | solution.py:21
  41.9 18.7 %collective-permute-start.15 = (bf16[192,384]{1,0:T(8,128)(2,1)S(1)}, bf16[192,384]{1,0:T(8,128)(2,1)}, u32[]{:S(2)}, u32[]{:S(2)}) collective-permute-start(bf16[192,384]{1,0:T(8,128)(2,1)S(1)} %bitcast.191), channel_id=1, source_target_pairs={{0,24},{8,16},{16,8},{24,0},{1,25},{9,17},{17,9},{25,1},{2,26},{10... | collective-permute-start | bytes 442376 | tf_op jit(solution)/shard_map/ppermute | solution.py:21
  55.8 17.8 %collective-permute-start.1 = (bf16[256,1536]{1,0:T(8,128)(2,1)S(1)}, bf16[256,1536]{1,0:T(8,128)(2,1)S(1)}, u32[]{:S(2)}, u32[]{:S(2)}) collective-permute-start(bf16[256,1536]{1,0:T(8,128)(2,1)S(1)} %bitcast.157), channel_id=1, source_target_pairs={{0,1},{1,0},{2,3},{3,2},{4,5},{5,4},{6,7},{7,6},{8,9},{9,8},{10,11... | collective-permute-start | bytes 2359304 | tf_op jit(solution)/shard_map/ppermute | solution.py:21
  59.2 9.7 %collective-permute-start.8 = (bf16[8,48,384]{2,1,0:T(8,128)(2,1)}, bf16[8,48,384]{2,1,0:T(8,128)(2,1)S(1)}, u32[]{:S(2)}, u32[]{:S(2)}) collective-permute-start(bf16[8,48,384]{2,1,0:T(8,128)(2,1)} %get-tuple-element.47), channel_id=1, source_target_pairs={{0,2},{1,3},{2,0},{3,1},{4,6},{5,7},{6,4},{7,5},{8,10},{9,11},{10,... | collective-permute-start | bytes 884744 | tf_op jit(solution)/shard_map/ppermute | solution.py:21
  61.6 7.5 %collective-permute-start.9 = (bf16[8,48,384]{2,1,0:T(8,128)(2,1)}, bf16[8,48,384]{2,1,0:T(8,128)(2,1)S(1)}, u32[]{:S(2)}, u32[]{:S(2)}) collective-permute-start(bf16[8,48,384]{2,1,0:T(8,128)(2,1)} %get-tuple-element.47), channel_id=1, source_target_pairs={{0,1},{1,0},{2,3},{3,2},{4,5},{5,4},{6,7},{7,6},{8,9},{9,8},{10,11... | collective-permute-start | bytes 884744 | tf_op jit(solution)/shard_map/ppermute | solution.py:21
  61.9 44.5 %collective-permute-start.16 = (bf16[4,192,384]{2,1,0:T(8,128)(2,1)S(1)}, bf16[4,192,384]{2,1,0:T(8,128)(2,1)S(1)}, u32[]{:S(2)}, u32[]{:S(2)}) collective-permute-start(bf16[4,192,384]{2,1,0:T(8,128)(2,1)S(1)} %pad_maximum_fusion.4.refs_0_), channel_id=1, source_target_pairs={{0,4},{4,0},{1,5},{5,1},{2,6},{6,2},{3,7},{7,3},{8,12},{12,8},{9,1... | collective-permute-start | bytes 1769480 | tf_op jit(solution)/shard_map/ppermute | solution.py:21
  64.7 8.9 %collective-permute-start.2 = (bf16[256,1536]{1,0:T(8,128)(2,1)S(1)}, bf16[256,1536]{1,0:T(8,128)(2,1)S(1)}, u32[]{:S(2)}, u32[]{:S(2)}) collective-permute-start(bf16[256,1536]{1,0:T(8,128)(2,1)S(1)} %collective-permute-done), channel_id=1, source_target_pairs={{0,1},{1,0},{2,3},{3,2},{4,5},{5,4},{6,7},{7,6},{8,9},{9,8},{10,11... | collective-permute-start | bytes 2359304 | tf_op jit(solution)/shard_map/ppermute | solution.py:21
  70.5 19.7 %collective-permute-start.11 = (bf16[256,1536]{1,0:T(8,128)(2,1)S(1)}, bf16[256,1536]{1,0:T(8,128)(2,1)}, u32[]{:S(2)}, u32[]{:S(2)}) collective-permute-start(bf16[256,1536]{1,0:T(8,128)(2,1)S(1)} %bitcast.150), channel_id=1, source_target_pairs={{0,2},{1,3},{2,0},{3,1},{4,6},{5,7},{6,4},{7,5},{8,10},{9,11},{10,... | collective-permute-start | bytes 2359304 | tf_op jit(solution)/shard_map/ppermute | solution.py:21
  81.1 15.8 %collective-permute-start.12 = (bf16[1024,256]{1,0:T(8,128)(2,1)S(1)}, bf16[1024,256]{1,0:T(8,128)(2,1)S(1)}, u32[]{:S(2)}, u32[]{:S(2)}) collective-permute-start(bf16[1024,256]{1,0:T(8,128)(2,1)S(1)} %convolution_convert_fusion.8.own_ref), channel_id=1, source_target_pairs={{0,4},{1,5},{2,6},{3,7},{8,12},{9,13},{10,14},{11,15},{16,20},{17,... | collective-permute-start | bytes 1572872 | tf_op jit(solution)/shard_map/ppermute | solution.py:27
  117.5 19.6 %collective-permute-start.18 = (bf16[256,1536]{1,0:T(8,128)(2,1)S(1)}, bf16[256,1536]{1,0:T(8,128)(2,1)S(1)}, u32[]{:S(2)}, u32[]{:S(2)}) collective-permute-start(bf16[256,1536]{1,0:T(8,128)(2,1)S(1)} %slice.292), channel_id=1, source_target_pairs={{0,2},{1,3},{2,0},{3,1},{4,6},{5,7},{6,4},{7,5},{8,10},{9,11},{10,... | collective-permute-start | bytes 2359304 | tf_op jit(solution)/shard_map/ppermute | solution.py:21
  137.8 19.0 %collective-permute-start.19 = (bf16[256,1536]{1,0:T(8,128)(2,1)S(1)}, bf16[256,1536]{1,0:T(8,128)(2,1)}, u32[]{:S(2)}, u32[]{:S(2)}) collective-permute-start(bf16[256,1536]{1,0:T(8,128)(2,1)S(1)} %multiply_convert_fusion.refs_0_), channel_id=1, source_target_pairs={{0,2},{1,3},{2,0},{3,1},{4,6},{5,7},{6,4},{7,5},{8,10},{9,11},{10,... | collective-permute-start | bytes 2359304 | tf_op jit(solution)/shard_map/ppermute | solution.py:21
  138.6 18.3 %collective-permute-start.22 = (bf16[256,1536]{1,0:T(8,128)(2,1)S(1)}, bf16[256,1536]{1,0:T(8,128)(2,1)}, u32[]{:S(2)}, u32[]{:S(2)}) collective-permute-start(bf16[256,1536]{1,0:T(8,128)(2,1)S(1)} %bitcast.151), channel_id=1, source_target_pairs={{0,1},{1,0},{2,3},{3,2},{4,5},{5,4},{6,7},{7,6},{8,9},{9,8},{10,11... | collective-permute-start | bytes 2359304 | tf_op jit(solution)/shard_map/ppermute | solution.py:21
  138.6 18.3 %collective-permute-start.23 = (bf16[256,1536]{1,0:T(8,128)(2,1)}, bf16[256,1536]{1,0:T(8,128)(2,1)}, u32[]{:S(2)}, u32[]{:S(2)}) collective-permute-start(bf16[256,1536]{1,0:T(8,128)(2,1)} %collective-permute-done.11.refs_5_), channel_id=1, source_target_pairs={{0,1},{1,0},{2,3},{3,2},{4,5},{5,4},{6,7},{7,6},{8,9},{9,8},{10,11... | collective-permute-start | bytes 2359304 | tf_op jit(solution)/shard_map/ppermute | solution.py:21
  139.1 17.8 %collective-permute-start.20 = (bf16[256,1536]{1,0:T(8,128)(2,1)S(1)}, bf16[256,1536]{1,0:T(8,128)(2,1)}, u32[]{:S(2)}, u32[]{:S(2)}) collective-permute-start(bf16[256,1536]{1,0:T(8,128)(2,1)S(1)} %multiply_convert_fusion.refs_0_), channel_id=1, source_target_pairs={{0,1},{1,0},{2,3},{3,2},{4,5},{5,4},{6,7},{7,6},{8,9},{9,8},{10,11... | collective-permute-start | bytes 2359304 | tf_op jit(solution)/shard_map/ppermute | solution.py:21
  218.7 40.3 %collective-permute-start.31 = (bf16[4,192,1152]{2,1,0:T(8,128)(2,1)}, bf16[4,192,1152]{2,1,0:T(8,128)(2,1)}, u32[]{:S(2)}, u32[]{:S(2)}) collective-permute-start(bf16[4,192,1152]{2,1,0:T(8,128)(2,1)} %dynamic-slice_bitcast_fusion.1), channel_id=1, source_target_pairs={{0,4},{4,0},{1,5},{5,1},{2,6},{6,2},{3,7},{7,3},{8,12},{12,8},{9,1... | collective-permute-start | bytes 5308424 | tf_op jit(solution)/shard_map/ppermute | solution.py:21
  237.9 12.9 %collective-permute-start.24 = (bf16[512,1536]{1,0:T(8,128)(2,1)S(1)}, bf16[512,1536]{1,0:T(8,128)(2,1)S(1)}, u32[]{:S(2)}, u32[]{:S(2)}) collective-permute-start(bf16[512,1536]{1,0:T(8,128)(2,1)S(1)} %fusion.16), channel_id=1, source_target_pairs={{0,1},{1,0},{2,3},{3,2},{4,5},{5,4},{6,7},{7,6},{8,9},{9,8},{10,11... | collective-permute-start | bytes 4718600 | tf_op jit(solution)/shard_map/ppermute | solution.py:21
  253.8 20.1 %collective-permute-start.25 = (bf16[256,1536]{1,0:T(8,128)(2,1)}, bf16[256,1536]{1,0:T(8,128)(2,1)S(1)}, u32[]{:S(2)}, u32[]{:S(2)}) collective-permute-start(bf16[256,1536]{1,0:T(8,128)(2,1)} %slice.291), channel_id=1, source_target_pairs={{0,2},{1,3},{2,0},{3,1},{4,6},{5,7},{6,4},{7,5},{8,10},{9,11},{10,... | collective-permute-start | bytes 2359304 | tf_op jit(solution)/shard_map/ppermute | solution.py:21
  262.3 170.1 %reduce-scatter.4.cloned.1.call-start = ((), (), s32[]{:S(2)}) async-start(), calls=%async_computation.4 | async-start | bytes 2211840 | tf_op jit(solution)/shard_map/reduce_scatter | solution.py:151
  265.3 40.4 %collective-permute-start.32 = (bf16[4,192,1152]{2,1,0:T(8,128)(2,1)}, bf16[4,192,1152]{2,1,0:T(8,128)(2,1)}, u32[]{:S(2)}, u32[]{:S(2)}) collective-permute-start(bf16[4,192,1152]{2,1,0:T(8,128)(2,1)} %dynamic-slice_bitcast_fusion.2), channel_id=1, source_target_pairs={{0,4},{4,0},{1,5},{5,1},{2,6},{6,2},{3,7},{7,3},{8,12},{12,8},{9,1... | collective-permute-start | bytes 5308424 | tf_op jit(solution)/shard_map/ppermute | solution.py:21
  280.2 19.3 %collective-permute-start.26 = (bf16[256,1536]{1,0:T(8,128)(2,1)S(1)}, bf16[256,1536]{1,0:T(8,128)(2,1)S(1)}, u32[]{:S(2)}, u32[]{:S(2)}) collective-permute-start(bf16[256,1536]{1,0:T(8,128)(2,1)S(1)} %get-tuple-element.107), channel_id=1, source_target_pairs={{0,2},{1,3},{2,0},{3,1},{4,6},{5,7},{6,4},{7,5},{8,10},{9,11},{10,... | collective-permute-start | bytes 2359304 | tf_op jit(solution)/shard_map/ppermute | solution.py:21
  289.3 20.2 %collective-permute-start.29 = (bf16[256,1536]{1,0:T(8,128)(2,1)S(1)}, bf16[256,1536]{1,0:T(8,128)(2,1)}, u32[]{:S(2)}, u32[]{:S(2)}) collective-permute-start(bf16[256,1536]{1,0:T(8,128)(2,1)S(1)} %get-tuple-element.107), channel_id=1, source_target_pairs={{0,1},{1,0},{2,3},{3,2},{4,5},{5,4},{6,7},{7,6},{8,9},{9,8},{10,11... | collective-permute-start | bytes 2359304 | tf_op jit(solution)/shard_map/ppermute | solution.py:21
  299.5 10.1 %collective-permute-start.30 = (bf16[256,1536]{1,0:T(8,128)(2,1)S(1)}, bf16[256,1536]{1,0:T(8,128)(2,1)}, u32[]{:S(2)}, u32[]{:S(2)}) collective-permute-start(bf16[256,1536]{1,0:T(8,128)(2,1)S(1)} %collective-permute-done.26), channel_id=1, source_target_pairs={{0,1},{1,0},{2,3},{3,2},{4,5},{5,4},{6,7},{7,6},{8,9},{9,8},{10,11... | collective-permute-start | bytes 2359304 | tf_op jit(solution)/shard_map/ppermute | solution.py:21
  305.2 41.5 %collective-permute-start.27 = (bf16[512,1536]{1,0:T(8,128)(2,1)}, bf16[512,1536]{1,0:T(8,128)(2,1)}, u32[]{:S(2)}, u32[]{:S(2)}) collective-permute-start(bf16[512,1536]{1,0:T(8,128)(2,1)} %fusion.13), channel_id=1, source_target_pairs={{0,1},{1,0},{2,3},{3,2},{4,5},{5,4},{6,7},{7,6},{8,9},{9,8},{10,11... | collective-permute-start | bytes 4718600 | tf_op jit(solution)/shard_map/ppermute | solution.py:21
  305.8 49.9 %collective-permute-start.38 = (bf16[4,192,1152]{2,1,0:T(8,128)(2,1)}, bf16[4,192,1152]{2,1,0:T(8,128)(2,1)}, u32[]{:S(2)}, u32[]{:S(2)}) collective-permute-start(bf16[4,192,1152]{2,1,0:T(8,128)(2,1)} %dynamic-slice_bitcast_fusion), channel_id=1, source_target_pairs={{0,4},{4,0},{1,5},{5,1},{2,6},{6,2},{3,7},{7,3},{8,12},{12,8},{9,1... | collective-permute-start | bytes 5308424 | tf_op jit(solution)/shard_map/ppermute | solution.py:21
  309.5 124.9 %reduce-scatter.6.cloned.1.call-start = ((), (), s32[]{:S(2)}) async-start(), calls=%async_computation.5 | async-start | bytes 2211840 | tf_op jit(solution)/shard_map/reduce_scatter | solution.py:151
  336.2 8.8 %collective-permute-start.36 = (bf16[256,512]{1,0:T(8,128)(2,1)S(1)}, bf16[256,512]{1,0:T(8,128)(2,1)S(1)}, u32[]{:S(2)}, u32[]{:S(2)}) collective-permute-start(bf16[256,512]{1,0:T(8,128)(2,1)S(1)} %slice.295), channel_id=1, source_target_pairs={{0,2},{1,3},{2,0},{3,1},{4,6},{5,7},{6,4},{7,5},{8,10},{9,11},{10,... | collective-permute-start | bytes 786440 | tf_op jit(solution)/shard_map/ppermute | solution.py:21
  340.0 25.9 %collective-permute-start.33 = (bf16[512,1536]{1,0:T(8,128)(2,1)}, bf16[512,1536]{1,0:T(8,128)(2,1)}, u32[]{:S(2)}, u32[]{:S(2)}) collective-permute-start(bf16[512,1536]{1,0:T(8,128)(2,1)} %convolution_convert_fusion.3), channel_id=1, source_target_pairs={{0,1},{1,0},{2,3},{3,2},{4,5},{5,4},{6,7},{7,6},{8,9},{9,8},{10,11... | collective-permute-start | bytes 4718600 | tf_op jit(solution)/shard_map/ppermute | solution.py:21
  345.1 8.9 %collective-permute-start.37 = (bf16[256,256]{1,0:T(8,128)(2,1)S(1)}, bf16[256,256]{1,0:T(8,128)(2,1)S(1)}, u32[]{:S(2)}, u32[]{:S(2)}) collective-permute-start(bf16[256,256]{1,0:T(8,128)(2,1)S(1)} %slice.296), channel_id=1, source_target_pairs={{4,0},{5,1},{6,2},{7,3},{12,8},{13,9},{14,10},{15,11},{20,16},{21,... | collective-permute-start | bytes 393224 | tf_op jit(solution)/shard_map/ppermute | solution.py:27
  352.5 20.0 %collective-permute-start.28 = (bf16[256,1536]{1,0:T(8,128)(2,1)}, bf16[256,1536]{1,0:T(8,128)(2,1)}, u32[]{:S(2)}, u32[]{:S(2)}) collective-permute-start(bf16[256,1536]{1,0:T(8,128)(2,1)} %slice.290), channel_id=1, source_target_pairs={{0,2},{1,3},{2,0},{3,1},{4,6},{5,7},{6,4},{7,5},{8,10},{9,11},{10,... | collective-permute-start | bytes 2359304 | tf_op jit(solution)/shard_map/ppermute | solution.py:21
  357.9 11.5 %collective-permute-start.40 = (bf16[2,8,48,384]{3,2,1,0:T(8,128)(2,1)}, bf16[2,8,48,384]{3,2,1,0:T(8,128)(2,1)}, u32[]{:S(2)}, u32[]{:S(2)}) collective-permute-start(bf16[2,8,48,384]{3,2,1,0:T(8,128)(2,1)} %slice.293), channel_id=1, source_target_pairs={{0,1},{1,0},{2,3},{3,2},{4,5},{5,4},{6,7},{7,6},{8,9},{9,8},{10,11... | collective-permute-start | bytes 1769480 | tf_op jit(solution)/shard_map/ppermute | solution.py:21
  357.9 47.4 %collective-permute-start.39 = (bf16[4,384,384]{2,1,0:T(8,128)(2,1)}, bf16[4,384,384]{2,1,0:T(8,128)(2,1)}, u32[]{:S(2)}, u32[]{:S(2)}) collective-permute-start(bf16[4,384,384]{2,1,0:T(8,128)(2,1)} %fusion.34), channel_id=1, source_target_pairs={{0,4},{4,0},{1,5},{5,1},{2,6},{6,2},{3,7},{7,3},{8,12},{12,8},{9,1... | collective-permute-start | bytes 3538952 | tf_op jit(solution)/shard_map/ppermute | solution.py:21
  368.5 29.1 %collective-permute-start.34 = (bf16[256,1536]{1,0:T(8,128)(2,1)S(1)}, bf16[256,1536]{1,0:T(8,128)(2,1)S(1)}, u32[]{:S(2)}, u32[]{:S(2)}) collective-permute-start(bf16[256,1536]{1,0:T(8,128)(2,1)S(1)} %slice.289), channel_id=1, source_target_pairs={{0,2},{1,3},{2,0},{3,1},{4,6},{5,7},{6,4},{7,5},{8,10},{9,11},{10,... | collective-permute-start | bytes 2359304 | tf_op jit(solution)/shard_map/ppermute | solution.py:21
  371.1 24.0 %collective-permute-start.41 = (bf16[1,8,48,384]{3,2,1,0:T(8,128)(2,1)S(1)}, bf16[1,8,48,384]{3,2,1,0:T(8,128)(2,1)S(1)}, u32[]{:S(2)}, u32[]{:S(2)}) collective-permute-start(bf16[1,8,48,384]{3,2,1,0:T(8,128)(2,1)S(1)} %slice.294), channel_id=1, source_target_pairs={{0,2},{1,3},{2,0},{3,1},{4,6},{5,7},{6,4},{7,5},{8,10},{9,11},{10,... | collective-permute-start | bytes 884744 | tf_op jit(solution)/shard_map/ppermute | solution.py:21
  400.9 6.9 %collective-permute-start.43 = (bf16[48,384]{1,0:T(8,128)(2,1)S(1)}, bf16[48,384]{1,0:T(8,128)(2,1)S(1)}, u32[]{:S(2)}, u32[]{:S(2)}) collective-permute-start(bf16[48,384]{1,0:T(8,128)(2,1)S(1)} %get-tuple-element.77), channel_id=1, source_target_pairs={{0,8},{8,0},{16,24},{24,16},{1,9},{9,1},{17,25},{25,17},{2,10},{10... | collective-permute-start | bytes 110600 | tf_op jit(solution)/shard_map/ppermute | solution.py:21
  400.9 6.8 %collective-permute-start.44 = (bf16[48,384]{1,0:T(8,128)(2,1)S(1)}, bf16[48,384]{1,0:T(8,128)(2,1)S(1)}, u32[]{:S(2)}, u32[]{:S(2)}) collective-permute-start(bf16[48,384]{1,0:T(8,128)(2,1)S(1)} %get-tuple-element.78), channel_id=1, source_target_pairs={{0,16},{8,24},{16,0},{24,8},{1,17},{9,25},{17,1},{25,9},{2,18},{10... | collective-permute-start | bytes 110600 | tf_op jit(solution)/shard_map/ppermute | solution.py:21
  403.1 5.9 %collective-permute-start.45 = (bf16[48,384]{1,0:T(8,128)(2,1)S(1)}, bf16[48,384]{1,0:T(8,128)(2,1)S(1)}, u32[]{:S(2)}, u32[]{:S(2)}) collective-permute-start(bf16[48,384]{1,0:T(8,128)(2,1)S(1)} %get-tuple-element.79), channel_id=1, source_target_pairs={{0,24},{8,16},{16,8},{24,0},{1,25},{9,17},{17,9},{25,1},{2,26},{10... | collective-permute-start | bytes 110600 | tf_op jit(solution)/shard_map/ppermute | solution.py:21
  409.0 13.3 %collective-permute-start.46 = (bf16[384,384]{1,0:T(8,128)(2,1)}, bf16[384,384]{1,0:T(8,128)(2,1)S(1)}, u32[]{:S(2)}, u32[]{:S(2)}) collective-permute-start(bf16[384,384]{1,0:T(8,128)(2,1)} %get-tuple-element.80), channel_id=1, source_target_pairs={{0,8},{8,0},{16,24},{24,16},{1,9},{9,1},{17,25},{25,17},{2,10},{10... | collective-permute-start | bytes 884744 | tf_op jit(solution)/shard_map/ppermute | solution.py:21
  409.0 22.4 %collective-permute-start.47 = (bf16[384,384]{1,0:T(8,128)(2,1)}, bf16[384,384]{1,0:T(8,128)(2,1)S(1)}, u32[]{:S(2)}, u32[]{:S(2)}) collective-permute-start(bf16[384,384]{1,0:T(8,128)(2,1)} %get-tuple-element.81), channel_id=1, source_target_pairs={{0,16},{8,24},{16,0},{24,8},{1,17},{9,25},{17,1},{25,9},{2,18},{10... | collective-permute-start | bytes 884744 | tf_op jit(solution)/shard_map/ppermute | solution.py:21
  411.8 19.6 %collective-permute-start.48 = (bf16[384,384]{1,0:T(8,128)(2,1)S(1)}, bf16[384,384]{1,0:T(8,128)(2,1)S(1)}, u32[]{:S(2)}, u32[]{:S(2)}) collective-permute-start(bf16[384,384]{1,0:T(8,128)(2,1)S(1)} %get-tuple-element.82), channel_id=1, source_target_pairs={{0,24},{8,16},{16,8},{24,0},{1,25},{9,17},{17,9},{25,1},{2,26},{10... | collective-permute-start | bytes 884744 | tf_op jit(solution)/shard_map/ppermute | solution.py:21
  (67 other events, 653.2 us)
Sparse Core Ops, SparseCore 0:
  29.3 163.1 all-gather.1
  262.4 36.9 reduce-scatter.7
  309.6 37.5 reduce-scatter.3
  363.9 36.0 reduce-scatter.5
